TPU v7x, 512 devices: a whole 4x4x16 slice. The times are simulated.
512 devices in a mesh: section: 16 (over x, z_hi), dp: 32 (over z_lo, y, core).
Axes of the slice: x: 4, y: 4, z: 16 (z_hi: 4, z_lo: 4; z = z_hi * 4 + z_lo), core: 2. Of those that a mesh axis runs over, the one named last changes fastest.
Arguments:
- hidden: bfloat16 [16, 64, 4096], P('section', 'dp'), may hold values from -16 to 16
- norm_gain: float32 [4096], replicated, may hold values from 0.5 to 2
- exit_head: bfloat16 [16384, 4096], P('dp', 'section'), may hold values from -4 to 4
- targets: int32 [64], replicated, may hold values from 0 to 16383
- loss_numerators: int32 [16], replicated, may hold values from 1 to 64
- top_grad: bfloat16 [64, 4096], P('dp'), may hold values from -8 to 8
Outputs:
- grad_head: bfloat16 [16384, 4096], P('dp', 'section')
- grad_hidden: bfloat16 [16, 64, 4096], P('section', 'dp')
All inputs are finite; a program needn't handle non-finite values.
Results may differ from a plain program's by a relative error of at most 0.0062.
Values may be sent and summed in bfloat16 or wider, within the bound.
A program may use at most 64 MiB of HBM per device.

v0:
```python
import jax
import jax.numpy as jnp
from jax import lax
from jax.sharding import PartitionSpec as P

EXIT_DENOM = 16


EPSILON = 1e-05


def joined(value, axis, join):
    pieces = jax.tree.map(lambda part: lax.all_gather(part, axis), value)
    head = jax.tree.map(lambda part: part[0], pieces)
    tail = jax.tree.map(lambda part: part[1:], pieces)
    total, _ = lax.scan(lambda total, section: (join(total, section), None), head, tail)
    return total


def passed_along(block, axis, distance):
    devices = range(lax.axis_size(axis))
    route = [(i - distance, i) for i in devices if i - distance in devices]
    return lax.ppermute(block, axis, route)


def combine_stats(first, second):
    peak_val = jnp.maximum(first[0], second[0])
    return (
        peak_val,
        first[1] * jnp.exp(first[0] - peak_val) + second[1] * jnp.exp(second[0] - peak_val),
    )


def local_stats(logits):
    peak_val = jnp.max(logits, axis=-1)
    return (peak_val, jnp.sum(jnp.exp(logits - peak_val[:, None]), axis=-1))


def softmax_grad(logits, peak_val, total_exp, row_scales, onehot):
    probs = jnp.exp(logits - peak_val[:, None]) / total_exp[:, None]
    return ((probs - onehot) * row_scales[:, None]).astype(jnp.bfloat16)


def body(hidden, norm_gain, exit_head, targets, loss_numerators, top_grad):
    sections = lax.axis_size("section")
    data_at = lax.axis_index("dp")
    local_rows = hidden.shape[1]
    vocab_part, feat_part = exit_head.shape
    hidden_f = hidden.astype(jnp.float32)
    inverse = lax.rsqrt(jnp.mean(hidden_f * hidden_f, axis=-1) + EPSILON)
    normed = (hidden_f * inverse[..., None] * norm_gain).astype(jnp.bfloat16)
    normed_feat = lax.all_to_all(normed, "section", split_axis=2, concat_axis=0, tiled=True)
    every_row = lax.all_gather(normed_feat, "dp", axis=1, tiled=True)
    total_rows = every_row.shape[1]
    per_block = min(sections, max(1, 512 // total_rows))
    block_size = per_block * total_rows
    flat_rows = every_row.reshape(sections * total_rows, feat_part)
    weights = loss_numerators.astype(jnp.float32) / EXIT_DENOM
    row_weights = jnp.repeat(weights, total_rows)
    first_id = data_at * vocab_part
    local_ids = targets - first_id
    onehot_rows = (local_ids[:, None] == jnp.arange(vocab_part, dtype=jnp.int32)[None, :]).astype(
        jnp.float32
    )
    onehot = jnp.tile(onehot_rows, (per_block, 1))

    def one_block(block_number, carry):
        grad_sum, feat_grads = carry
        row_start = block_number * block_size
        row_block = lax.dynamic_slice_in_dim(flat_rows, row_start, block_size, 0)
        row_scales = lax.dynamic_slice_in_dim(row_weights, row_start, block_size, 0)
        partial_logits = lax.dot_general(
            row_block, exit_head, (((1,), (1,)), ((), ())), preferred_element_type=jnp.float32
        )
        logits = lax.psum(partial_logits, "section")
        peak_val, total_exp = joined(local_stats(logits), "dp", combine_stats)
        dlogits = softmax_grad(logits, peak_val, total_exp, row_scales, onehot)
        grad_sum = grad_sum + lax.dot_general(
            dlogits, row_block, (((0,), (0,)), ((), ())), preferred_element_type=jnp.float32
        )
        feat_back = jnp.dot(dlogits, exit_head, preferred_element_type=jnp.float32).reshape(
            per_block, total_rows, feat_part
        )
        own_part = lax.psum_scatter(feat_back, "dp", scatter_dimension=1, tiled=True)
        feat_grads = lax.dynamic_update_slice_in_dim(
            feat_grads, own_part, block_number * per_block, 0
        )
        return (grad_sum, feat_grads)

    start_carry = (
        jnp.zeros((vocab_part, feat_part), jnp.float32),
        jnp.zeros((sections, local_rows, feat_part), jnp.float32),
    )
    grad_sum, feat_grads = lax.fori_loop(0, sections // per_block, one_block, start_carry)
    own_grads = lax.all_to_all(feat_grads, "section", split_axis=0, concat_axis=2, tiled=True)
    row_dots = jnp.mean(own_grads * norm_gain * hidden_f, axis=-1)
    exit_grads = inverse[..., None] * (
        norm_gain * own_grads - hidden_f * (inverse * inverse * row_dots)[..., None]
    )

    def relay_step(step_number, running):
        return exit_grads + passed_along(running, "section", -1)

    later_sum = lax.fori_loop(0, sections - 1, relay_step, exit_grads)
    result_grad = later_sum + top_grad.astype(jnp.float32)[None]
    return (grad_sum.astype(jnp.bfloat16), result_grad.astype(jnp.bfloat16))


def solution(mesh):
    placed = (P("section", "dp", None), P(), P("dp", "section"), P(), P(), P("dp", None))
    return jax.shard_map(
        body,
        mesh=mesh,
        in_specs=placed,
        out_specs=(P("dp", "section"), P("section", "dp", None)),
        check_vma=False,
    )
```

profile of v0, /device:TPU:6, one launch (start us, length us, event | category | flops | bytes accessed | tf_op | source)
XLA Modules:
  0.0 1180.1 jit_solution(17369333567686939319)
XLA Ops:
  7.2 0.9 fusion.10
  8.0 0.8 fusion.12
  8.9 2.7 copy.51
  12.1 22.4 %reduce.2 = bf16[4096,2]{1,0:T(8,128)(2,1)S(1)} reduce(bf16[4096,1,2]{2,1,0:T(2,128)(2,1)S(1)} %bitcast.75, bf16[]{:T(256)} %broadcast.99), dimensions={1}, to_apply=%bitcast.35.reduce_sub_computation | reduce | bytes 32770
  34.6 2.2 reshape.137
  36.8 18.0 %all-to-all-start = ((bf16[16,2,256]{2,1,0:T(2,128)(2,1)}), bf16[16,2,256]{2,1,0:T(2,128)(2,1)S(1)}, u32[]{:S(2)}, u32[]{:S(2)}) async-start(bf16[16,2,256]{2,1,0:T(2,128)(2,1)} %reshape.137), calls=%async_computation.1 | async-start | bytes 32768 | tf_op jit(solution)/shard_map/all_to_all | solution.py:52
  55.1 12.5 %all-to-all-done = bf16[16,2,256]{2,1,0:T(2,128)(2,1)S(1)} async-done(((bf16[16,2,256]{2,1,0:T(2,128)(2,1)}), bf16[16,2,256]{2,1,0:T(2,128)(2,1)S(1)}, u32[]{:S(2)}, u32[]{:S(2)}) %all-to-all-start) | async-done | bytes 16416 | tf_op jit(solution)/shard_map/all_to_all | solution.py:52
  67.6 2.4 reshape.138
  70.1 2.0 copy.52
  72.1 43.3 %all-gather.2 = bf16[16,1,64,256]{3,0,1,2:T(8,128)(2,1)S(1)} all-gather(bf16[16,1,2,256]{3,0,1,2:T(8,128)(2,1)S(1)} %bitcast.88), channel_id=4, replica_groups=mesh['section'=16,'dp'=32] {'dp'}, dimensions={2}, use_global_device_ids=true | all-gather | bytes 540672 | tf_op jit(solution)/shard_map/all_gather | solution.py:53
  116.2 876.4 %while.57 = (s32[]{:T(128)}, f32[512,256]{1,0:T(8,128)S(1)}, f32[16,2,256]{2,1,0:T(2,128)}, bf16[1024,256]{1,0:T(8,128)(2,1)S(1)}, bf16[512,256]{1,0:T(8,128)(2,...) while((s32[]{:T(128)}, f32[512,256]{1,0:T(8,128)S(1)}, ...), condition=%wide.region_8.9_spmd.clone, body=%wide.region_1.8_spmd.clone.sunk | while | flops 405276672 | bytes 22397424 | solution.py:94
  116.3 1.4 fusion.37
  117.8 202.1 %all-reduce.2.cloned.1.call-done = f32[512,512]{1,0:T(8,128)} async-done(((f32[512,512]{1,0:T(8,128)}), f32[512,512]{1,0:T(8,128)}) %all-reduce.2.cloned.1.call-update) | async-done | bytes 1048592 | tf_op jit(solution)/shard_map/while/body/eval_jaxpr/psum | solution.py:75
  319.9 1.5 reduce_max.15
  321.4 1.5 exponential_reduce_fusion.2
  322.9 40.4 %all-gather.10 = f32[32,1,512]{2,1,0:T(1,128)S(1)} all-gather(f32[1,1,512]{2,1,0:T(1,128)S(1)} %bitcast.86), channel_id=3, replica_groups=mesh['section'=16,'dp'=32] {'dp'}, dimensions={0}, use_global_device_ids=true | all-gather | bytes 67584 | tf_op jit(solution)/shard_map/while/body/eval_jaxpr/all_gather | solution.py:13
  363.3 38.1 %all-gather.9 = f32[32,1,512]{2,1,0:T(1,128)S(1)} all-gather(f32[1,1,512]{2,1,0:T(1,128)S(1)} %bitcast.83), channel_id=2, replica_groups=mesh['section'=16,'dp'=32] {'dp'}, dimensions={0}, use_global_device_ids=true | all-gather | bytes 67584 | tf_op jit(solution)/shard_map/while/body/eval_jaxpr/all_gather | solution.py:13
  401.4 1.7 while.58
  403.7 1.1 copy.77
  405.3 143.8 %reduce-scatter.2.cloned.1.call-done = f32[8,2,256]{2,0,1:T(8,128)} async-done(((f32[8,64,256]{2,0,1:T(8,128)}), f32[8,2,256]{2,0,1:T(8,128)}) %reduce-scatter.2.cloned.1.call-update) | async-done | bytes 16400 | tf_op jit(solution)/shard_map/while/body/eval_jaxpr/reduce_scatter | solution.py:84
  549.0 1.3 copy_dynamic-update-slice_fusion.2
  550.4 1.3 fusion.37
  551.9 209.8 %all-reduce.2.cloned.1.call-done = f32[512,512]{1,0:T(8,128)} async-done(((f32[512,512]{1,0:T(8,128)}), f32[512,512]{1,0:T(8,128)}) %all-reduce.2.cloned.1.call-update) | async-done | bytes 1048592 | tf_op jit(solution)/shard_map/while/body/eval_jaxpr/psum | solution.py:75
  761.6 1.5 reduce_max.15
  763.1 1.5 exponential_reduce_fusion.2
  764.6 41.0 %all-gather.10 = f32[32,1,512]{2,1,0:T(1,128)S(1)} all-gather(f32[1,1,512]{2,1,0:T(1,128)S(1)} %bitcast.86), channel_id=3, replica_groups=mesh['section'=16,'dp'=32] {'dp'}, dimensions={0}, use_global_device_ids=true | all-gather | bytes 67584 | tf_op jit(solution)/shard_map/while/body/eval_jaxpr/all_gather | solution.py:13
  805.6 38.1 %all-gather.9 = f32[32,1,512]{2,1,0:T(1,128)S(1)} all-gather(f32[1,1,512]{2,1,0:T(1,128)S(1)} %bitcast.83), channel_id=2, replica_groups=mesh['section'=16,'dp'=32] {'dp'}, dimensions={0}, use_global_device_ids=true | all-gather | bytes 67584 | tf_op jit(solution)/shard_map/while/body/eval_jaxpr/all_gather | solution.py:13
  843.7 1.7 while.58
  846.0 1.1 copy.77
  847.6 143.7 %reduce-scatter.2.cloned.1.call-done = f32[8,2,256]{2,0,1:T(8,128)} async-done(((f32[8,64,256]{2,0,1:T(8,128)}), f32[8,2,256]{2,0,1:T(8,128)}) %reduce-scatter.2.cloned.1.call-update) | async-done | bytes 16400 | tf_op jit(solution)/shard_map/while/body/eval_jaxpr/reduce_scatter | solution.py:84
  991.3 1.3 copy_dynamic-update-slice_fusion.2
  992.6 12.6 %all-to-all-start.1 = ((f32[16,2,256]{2,1,0:T(2,128)}), f32[16,2,256]{2,1,0:T(2,128)S(1)}, u32[]{:S(2)}, u32[]{:S(2)}) async-start(f32[16,2,256]{2,1,0:T(2,128)} %get-tuple-element.173), calls=%async_computation.2 | async-start | bytes 65536 | tf_op jit(solution)/shard_map/all_to_all | solution.py:95
  1005.9 12.1 %all-to-all-done.1 = f32[16,2,256]{2,1,0:T(2,128)S(1)} async-done(((f32[16,2,256]{2,1,0:T(2,128)}), f32[16,2,256]{2,1,0:T(2,128)S(1)}, u32[]{:S(2)}, u32[]{:S(2)}) %all-to-all-start.1) | async-done | bytes 32800 | tf_op jit(solution)/shard_map/all_to_all | solution.py:95
  1018.3 154.6 %while.55 = (s32[]{:T(128)}, f32[1,2,4096]{2,1,0:T(2,128)S(1)}, f32[1,2,4096]{2,1,0:T(2,128)S(1)}, s32[]{:T(128)}) while((s32[]{:T(128)}, f32[1,2,4096]{2,1,0:T(2,128)S(1)}, f32[1,2,4096]{2,1,0:T(2,128)S(1)}, s32[]{:T(128)}) %tuple.81), condition=%wide.region_11.12_spmd, body=%wide.region_10.11_spmd.sunk | while | flops 8194 | bytes 229469 | solution.py:104
  1018.3 2.7 collective-permute-start
  1021.0 7.5 collective-permute-done
  1028.6 3.1 collective-permute-start
  1031.7 7.9 collective-permute-done
  1039.6 2.7 collective-permute-start
  1042.3 7.3 collective-permute-done
  1049.6 3.7 collective-permute-start
  1053.3 6.5 collective-permute-done
  1059.8 4.8 collective-permute-start
  1064.6 4.9 collective-permute-done
  1069.6 5.7 collective-permute-start
  1075.3 4.0 collective-permute-done
  1079.3 6.6 collective-permute-start
  1086.0 3.1 collective-permute-done
  1089.1 7.5 collective-permute-start
  1096.6 2.2 collective-permute-done
  1098.9 8.4 collective-permute-start
  1107.3 1.6 collective-permute-done
  1108.9 9.1 collective-permute-start
  1118.0 1.6 collective-permute-done
  1119.6 9.0 collective-permute-start
  1128.7 1.6 collective-permute-done
  1130.3 9.0 collective-permute-start
  1139.3 1.6 collective-permute-done
  1140.9 9.0 collective-permute-start
  1150.0 1.6 collective-permute-done
  1151.6 9.0 collective-permute-start
  1160.6 1.6 collective-permute-done
  1162.2 9.0 collective-permute-start
  1171.3 1.6 collective-permute-done
  (200 shorter events, 8.0 us)
Async XLA Ops:
  12.1 42.7 %copy-start.5 = (s32[64]{0:T(128)S(1)}, s32[64]{0:T(128)}, u32[]{:S(2)}) copy-start(s32[64]{0:T(128)} %param.15) | copy-start | bytes 772
  12.1 42.8 %copy-start.6 = (s32[16]{0:T(128)S(1)}, s32[16]{0:T(128)}, u32[]{:S(2)}) copy-start(s32[16]{0:T(128)} %param.16) | copy-start | bytes 196
  36.8 30.9 %all-to-all-start = ((bf16[16,2,256]{2,1,0:T(2,128)(2,1)}), bf16[16,2,256]{2,1,0:T(2,128)(2,1)S(1)}, u32[]{:S(2)}, u32[]{:S(2)}) async-start(bf16[16,2,256]{2,1,0:T(2,128)(2,1)} %reshape.137), calls=%async_computation.1 | async-start | bytes 32768 | tf_op jit(solution)/shard_map/all_to_all | solution.py:52
  70.1 46.1 %copy-start.1 = (bf16[512,256]{1,0:T(8,128)(2,1)S(1)}, bf16[512,256]{1,0:T(8,128)(2,1)}, u32[]{:S(2)}) copy-start(bf16[512,256]{1,0:T(8,128)(2,1)} %param.14) | copy-start | bytes 786436
  116.2 901.9 %copy-start.2 = (bf16[1,2,4096]{2,1,0:T(2,128)(2,1)S(1)}, bf16[1,2,4096]{2,1,0:T(2,128)(2,1)}, u32[]{:S(2)}) copy-start(bf16[1,2,4096]{2,1,0:T(2,128)(2,1)} %param.12) | copy-start | bytes 49156
  116.2 901.9 %copy-start.3 = (f32[4096]{0:T(1024)S(1)}, f32[4096]{0:T(1024)}, u32[]{:S(2)}) copy-start(f32[4096]{0:T(1024)} %param.13) | copy-start | bytes 49156
  116.2 1056.7 %copy-start.4 = (bf16[2,4096]{1,0:T(2,128)(2,1)S(1)}, bf16[2,4096]{1,0:T(2,128)(2,1)}, u32[]{:S(2)}) copy-start(bf16[2,4096]{1,0:T(2,128)(2,1)} %param.17) | copy-start | bytes 49156
  116.2 203.7 %all-reduce.2.cloned.1.call-start = ((), (), s32[]{:S(2)}) async-start(), calls=%async_computation.3 | async-start | bytes 2097152 | tf_op jit(solution)/shard_map/while/body/eval_jaxpr/psum | solution.py:75
  117.6 431.4 %reduce-scatter.2.cloned.1.call-start = ((), (), s32[]{:S(2)}) async-start(), calls=%async_computation.4 | async-start | bytes 540672 | tf_op jit(solution)/shard_map/while/body/eval_jaxpr/reduce_scatter | solution.py:84
  319.9 83.1 %copy-start = (f32[512,512]{1,0:T(8,128)S(1)}, f32[512,512]{1,0:T(8,128)}, u32[]{:S(2)}) copy-start(f32[512,512]{1,0:T(8,128)} %all-reduce.2.cloned.1.call-done) | copy-start | bytes 3145732 | tf_op jit(solution)/shard_map/while
  550.4 211.3 %all-reduce.2.cloned.1.call-start = ((), (), s32[]{:S(2)}) async-start(), calls=%async_computation.3 | async-start | bytes 2097152 | tf_op jit(solution)/shard_map/while/body/eval_jaxpr/psum | solution.py:75
  551.7 439.5 %reduce-scatter.2.cloned.1.call-start = ((), (), s32[]{:S(2)}) async-start(), calls=%async_computation.4 | async-start | bytes 540672 | tf_op jit(solution)/shard_map/while/body/eval_jaxpr/reduce_scatter | solution.py:84
  761.6 83.7 %copy-start = (f32[512,512]{1,0:T(8,128)S(1)}, f32[512,512]{1,0:T(8,128)}, u32[]{:S(2)}) copy-start(f32[512,512]{1,0:T(8,128)} %all-reduce.2.cloned.1.call-done) | copy-start | bytes 3145732 | tf_op jit(solution)/shard_map/while
  992.6 25.5 %all-to-all-start.1 = ((f32[16,2,256]{2,1,0:T(2,128)}), f32[16,2,256]{2,1,0:T(2,128)S(1)}, u32[]{:S(2)}, u32[]{:S(2)}) async-start(f32[16,2,256]{2,1,0:T(2,128)} %get-tuple-element.173), calls=%async_computation.2 | async-start | bytes 65536 | tf_op jit(solution)/shard_map/all_to_all | solution.py:95
  1018.3 10.2 collective-permute-start
  1028.6 11.0 collective-permute-start
  1039.6 10.0 collective-permute-start
  1049.6 10.2 collective-permute-start
  1059.8 9.7 collective-permute-start
  1069.6 9.7 collective-permute-start
  1079.3 9.7 collective-permute-start
  1089.1 9.7 collective-permute-start
  1098.9 10.0 collective-permute-start
  1108.9 10.7 collective-permute-start
  1119.6 10.6 collective-permute-start
  1130.3 10.6 collective-permute-start
  1140.9 10.6 collective-permute-start
  1151.6 10.6 collective-permute-start
  1162.2 10.6 collective-permute-start
Sparse Core Ops, SparseCore 0:
  120.0 199.9 all-reduce.1
  404.9 144.0 reduce-scatter.1
  554.1 207.4 all-reduce.1
  847.2 143.9 reduce-scatter.1
where the time goes:
time: 1180 us
  waiting for transfers between devices  778 us (66%)
  blocking collectives  201 us (17%)
  starting transfers between devices  130 us (11%)
  other arithmetic  34 us (3%)
  local copies, waits for them, and re-layouts  16.6 us (1%)
  between operations  13.8 us (1%)
    psum x2, waiting for transfers between devices, one_block(): logits = lax.psum(partial_logits, 'section')  412 us
    reduce_scatter x2, waiting for transfers between devices, one_block(): lax.psum_scatter(feat_back, 'dp', scatter_dimension=1, tiled=True)  287 us
    all_gather x4, blocking collectives, joined(): pieces = jax.tree.map(lambda part: lax.all_gather(part, axis), value)  157 us
    ppermute x15, starting transfers between devices, passed_along(): return lax.ppermute(block, axis, route)  99.5 us
    ppermute x15, waiting for transfers between devices, passed_along(): return lax.ppermute(block, axis, route)  54.4 us
    all_gather x1, blocking collectives, body(): every_row = lax.all_gather(normed_feat, 'dp', axis=1, tiled=True)  43.3 us
  transfers between devices with their start and end apart: 21, of which 21 were waited for; matrix products, arithmetic and copies ran while one was open for 0% of the time, Pallas kernels for 0%

commit v1 on v0

v1 whole, which is shorter than its diff:
```python
import functools

import jax
import jax.numpy as jnp
from jax import lax
from jax.experimental import pallas as pl
from jax.experimental.pallas import tpu as pltpu
from jax.sharding import PartitionSpec as P

MESH = pl.DeviceIdType.MESH
EXIT_DENOM = 16
EPSILON = 1e-05
F32 = jnp.float32
BF16 = jnp.bfloat16
D = 4096
HALF = D // 2
COPIES = 128


def dot(a, b, contract):
    return lax.dot_general(a, b, (contract, ((), ())), preferred_element_type=F32)


def kernel(
    hidden_ref, gain_ref, head_ref, targets_ref, nums_ref, top_ref,
    ghead_ref, ghid_ref,
    hid, hid8, inv8, n8, norm, heads, logits, stats, dlog_t, dlog_2, feat, grad,
    fs_far, fr_far, fs_near, fr_near, ws, wr, ts, tr, sf, cs, cr,
    gs_far, gr_far, gs_near, gr_near, gs_z, gq,
    ssem, rsem,
):
    sec, dp = lax.axis_index("section"), lax.axis_index("dp")
    x, h = sec // 4, sec % 4
    l, y, c = dp // 8, (dp // 2) % 4, dp % 2
    z = 4 * h + l

    def dev(dx=0, dy=0, dz=0, flip=False):
        nx, ny, nz = (x + dx) % 4, (y + dy) % 4, (z + dz) % 16
        nc = 1 - c if flip else c
        return {"section": nx * 4 + nz // 4, "dp": (nz % 4) * 8 + ny * 2 + nc}

    copies = []

    def push(src, dst, where):
        i = len(copies)
        copy = pltpu.make_async_remote_copy(
            src_ref=src, dst_ref=dst, send_sem=ssem.at[i], recv_sem=rsem.at[i],
            device_id=where, device_id_type=MESH,
        )
        copy.start()
        copies.append(copy)
        return copy

    Z_WINDOW = (1, 15, 2)
    Z_CLASS = (4, 12, 8)
    barrier = pltpu.get_barrier_semaphore()
    partners = [dev(dz=k) for k in (1, 15, 2, 14, 4, 12, 8)]
    partners += [dev(dy=k) for k in (1, 2, 3)] + [dev(dx=k) for k in (1, 2, 3)] + [dev(flip=True)]
    for where in partners:
        pl.semaphore_signal(barrier, inc=1, device_id=where, device_id_type=MESH)
    pl.semaphore_wait(barrier, len(partners))

    hid_in = [push(hidden_ref.at[0], hid.at[h], dev(dz=k)) for k in Z_CLASS]
    mine = pl.ds(pl.multiple_of(c * 128, 128), 128)
    mine_a = pl.ds(pl.multiple_of(c * 128, 64), 64)
    mine_b = pl.ds(pl.multiple_of(c * 128 + 64, 64), 64)
    other = pl.ds(pl.multiple_of((1 - c) * 128, 128), 128)
    head_in = []
    for k in Z_CLASS:
        quarter = pl.multiple_of(((h + k // 4) % 4) * 128, 128)
        head_in.append(push(head_ref.at[pl.ds(quarter, 128)], heads.at[x, h, mine], dev(dz=k)))
    heads[x, h, mine] = head_ref[pl.ds(pl.multiple_of(h * 128, 128), 128), :]
    hid[h] = hidden_ref[0]

    from_left, from_right, core_in = [], [], []

    def spread(hh):
        block = heads.at[x, hh, mine]
        from_left.append(push(block, block, dev(dx=1)))
        from_right.append(push(block, block, dev(dx=-1)))
        core_in.append(push(block, block, dev(flip=True)))

    spread(h)

    lane = lax.broadcasted_iota(jnp.int32, (1, 128), 1)
    lane_y, lane_l, lane_h, lane_r = lane // 32, (lane // 8) % 4, (lane // 2) % 4, lane % 2
    row_of = lane_l * 16 + lane_y * 4 + lane_r
    target = jnp.zeros((1, 128), jnp.int32)
    for k in range(64):
        if (k // 2) % 2 == 0:
            target = jnp.where(row_of == k, targets_ref[k + 2 * c], target)
    weight = jnp.zeros((1, 128), F32)
    for k in range(4):
        weight = jnp.where(lane_h == k, nums_ref[x * 4 + k].astype(F32) / EXIT_DENOM, weight)

    for copy in hid_in:
        copy.wait_recv()
    gain = gain_ref[...]
    rows8 = jnp.concatenate([hid[k].astype(F32) for k in range(4)], axis=0)
    inverse = lax.rsqrt(jnp.mean(rows8 * rows8, axis=-1, keepdims=True) + EPSILON)
    hid8[...] = rows8
    inv8[...] = jnp.broadcast_to(inverse, (8, 128))
    n8[l] = (rows8 * inverse * gain).astype(BF16)
    window_in = [push(n8.at[l], n8.at[l], dev(dz=k)) for k in Z_WINDOW]

    def norm_rows(yy):
        return pl.ds(pl.multiple_of(c * 128 + yy * 32, 32), 32)

    for copy in window_in:
        copy.wait_recv()
    norm[norm_rows(y), :] = jnp.concatenate([n8[k].astype(F32) for k in range(4)], axis=0).astype(BF16)
    cols_a, cols_b = pl.ds(0, HALF), pl.ds(HALF, HALF)
    own_a, own_b = norm.at[norm_rows(y), cols_a], norm.at[norm_rows(y), cols_b]
    down_a = push(own_a, own_a, dev(dy=1))
    up_b = push(own_b, own_b, dev(dy=-1))
    down_b = push(own_b, own_b, dev(dy=1))
    up_a = push(own_a, own_a, dev(dy=-1))
    norm_core = [push(norm.at[norm_rows(y)], norm.at[norm_rows(y)], dev(flip=True))]

    order = [h] + [(h - k // 4) % 4 for k in Z_CLASS]
    for copy, hh in zip(head_in, order[1:]):
        copy.wait_recv()
        spread(hh)
    down_a.wait_recv()
    past = norm.at[norm_rows((y - 1) % 4), cols_a]
    far_a = push(past, past, dev(dy=1))
    up_b.wait_recv()
    past = norm.at[norm_rows((y + 1) % 4), cols_b]
    far_b = push(past, past, dev(dy=-1))
    far_head = []
    for k, hh in enumerate(order):
        from_left[k].wait_recv()
        part = heads.at[(x - 1) % 4, hh, mine_a]
        one = push(part, part, dev(dx=1))
        block = heads.at[(x - 1) % 4, hh, mine]
        core_in.append(push(block, block, dev(flip=True)))
        from_right[k].wait_recv()
        part = heads.at[(x + 1) % 4, hh, mine_b]
        two = push(part, part, dev(dx=-1))
        block = heads.at[(x + 1) % 4, hh, mine]
        core_in.append(push(block, block, dev(flip=True)))
        far_head.append((one, two))
    for pair, dy in (((down_b,), -1), ((up_a,), 1), ((far_a, far_b), 2)):
        for copy in pair:
            copy.wait_recv()
        block = norm.at[norm_rows((y + dy) % 4)]
        norm_core.append(push(block, block, dev(flip=True)))
    for (one, two), hh in zip(far_head, order):
        one.wait_recv()
        two.wait_recv()
        block = heads.at[(x + 2) % 4, hh, mine]
        core_in.append(push(block, block, dev(flip=True)))
    for copy in core_in:
        copy.wait_recv()

    tokens = pl.ds(pl.multiple_of(c * 128, 128), 128)
    logits[...] = jnp.zeros((256, 128), F32)

    def add_block(k, carry):
        cols = pl.ds(pl.multiple_of(k * 256, 256), 256)
        logits[...] += dot(heads[k // 4, k % 4], norm[tokens, cols], ((1,), (1,)))
        return carry

    lax.fori_loop(0, 16, add_block, 0)
    values = logits[...]
    peak = jnp.max(values, axis=0, keepdims=True)
    expo = jnp.exp(values - peak)
    total = jnp.sum(expo, axis=0, keepdims=True)
    first_peak = peak
    pad = jnp.zeros((6, 128), F32)
    stages = ([dev(dy=k) for k in (1, 3, 2)], [dev(dz=k) for k in Z_WINDOW], [dev(dz=k) for k in Z_CLASS])
    for stage, peers in enumerate(stages):
        stats[stage, 3] = jnp.concatenate([peak, total, pad], axis=0)
        arrivals = [push(stats.at[stage, 3], stats.at[stage, k], peer) for k, peer in enumerate(peers)]
        for copy in arrivals:
            copy.wait_recv()
        parts = [stats[stage, k] for k in range(4)]
        peak = functools.reduce(jnp.maximum, [part[0:1] for part in parts])
        total = sum(part[1:2] * jnp.exp(part[0:1] - peak) for part in parts)

    row = lax.broadcasted_iota(jnp.int32, (256, 128), 0)
    vocab_id = 512 * (2 * (l * 4 + y) + row // 128) + 128 * h + row % 128
    onehot = jnp.where(vocab_id == target, 1.0, 0.0)
    dlog = weight * (expo * (jnp.exp(first_peak - peak) / total) - onehot)
    dlog_t[...] = dlog.astype(BF16)
    dlog_in = push(dlog_t.at[other], dlog_2.at[c], dev(flip=True))
    dlog_2[c] = dlog_t[mine, :]
    dlog_n = dlog.T.astype(BF16)

    def feat_block(k, carry):
        cols = pl.ds(pl.multiple_of(k * 256, 256), 256)
        feat[:, cols] = dot(dlog_n, heads[k // 4, k % 4], ((1,), (0,)))
        return carry

    lax.fori_loop(0, 16, feat_block, 0)

    def feat_rows(dy):
        return pl.ds(pl.multiple_of(((y + dy) % 4) * 32, 32), 32)

    fs_far[0] = feat[feat_rows(2), cols_a].astype(BF16)
    fs_far[1] = feat[feat_rows(2), cols_b].astype(BF16)
    feat_far = [push(fs_far.at[0], fr_far.at[0], dev(dy=1)), push(fs_far.at[1], fr_far.at[1], dev(dy=-1))]
    fs_near[1] = feat[feat_rows(1), cols_b].astype(BF16)
    fs_near[2] = feat[feat_rows(-1), cols_a].astype(BF16)
    feat_near = [push(fs_near.at[1], fr_near.at[1], dev(dy=1)), push(fs_near.at[2], fr_near.at[2], dev(dy=-1))]

    dlog_in.wait_recv()
    for copy in norm_core:
        copy.wait_recv()
    dlog_all = jnp.concatenate([dlog_2[0], dlog_2[1]], axis=1)
    grad_order = [(h + k // 4) % 4 for k in (8, 4, 12, 0)]
    grad_far, grad_near = [], []
    for j, hh in enumerate(grad_order):
        def grad_block(k, carry, hh=hh):
            cols = pl.ds(pl.multiple_of((k * 4 + hh) * 256, 256), 256)
            grad[k, hh] = dot(dlog_all, norm[:, cols], ((1,), (0,)))
            return carry

        lax.fori_loop(0, 4, grad_block, 0)
        far = grad.at[(x + 2) % 4, hh]
        gs_far[j, 0] = far[0:64].astype(BF16)
        gs_far[j, 1] = far[64:128].astype(BF16)
        grad_far.append((
            push(gs_far.at[j, 0], gr_far.at[j, 0], dev(dx=1)),
            push(gs_far.at[j, 1], gr_far.at[j, 1], dev(dx=-1)),
        ))
        gs_near[j, 1] = grad.at[(x + 1) % 4, hh][64:128].astype(BF16)
        gs_near[j, 2] = grad.at[(x - 1) % 4, hh][0:64].astype(BF16)
        grad_near.append([
            push(gs_near.at[j, 1], gr_near.at[j, 1], dev(dx=1)),
            push(gs_near.at[j, 2], gr_near.at[j, 2], dev(dx=-1)),
        ])

    feat_far[0].wait_recv()
    fs_near[0] = (feat[feat_rows(1), cols_a] + fr_far[0].astype(F32)).astype(BF16)
    feat_near.append(push(fs_near.at[0], fr_near.at[0], dev(dy=1)))
    feat_far[1].wait_recv()
    fs_near[3] = (feat[feat_rows(-1), cols_b] + fr_far[1].astype(F32)).astype(BF16)
    feat_near.append(push(fs_near.at[3], fr_near.at[3], dev(dy=-1)))

    for j, hh in enumerate(grad_order):
        grad_far[j][0].wait_recv()
        gs_near[j, 0] = (grad.at[(x + 1) % 4, hh][0:64] + gr_far[j, 0].astype(F32)).astype(BF16)
        grad_near[j].append(push(gs_near.at[j, 0], gr_near.at[j, 0], dev(dx=1)))
        grad_far[j][1].wait_recv()
        gs_near[j, 3] = (grad.at[(x - 1) % 4, hh][64:128] + gr_far[j, 1].astype(F32)).astype(BF16)
        grad_near[j].append(push(gs_near.at[j, 3], gr_near.at[j, 3], dev(dx=-1)))

    for copy in feat_near:
        copy.wait_recv()
    near = [fr_near[k].astype(F32) for k in range(4)]
    summed = feat[feat_rows(0), :] + jnp.concatenate([near[0] + near[2], near[1] + near[3]], axis=1)
    feat[feat_rows(0), :] = summed
    for k in range(4):
        ws[k] = summed[8 * k : 8 * k + 8].astype(BF16)
    feat_window = [push(ws.at[(l + k) % 4], wr.at[i], dev(dz=k)) for i, k in enumerate(Z_WINDOW)]

    grad_z = []

    def finish_grad(j):
        hh = grad_order[j]
        for copy in grad_near[j]:
            copy.wait_recv()
        part = [gr_near[j, k].astype(F32) for k in range(4)]
        whole = grad[x, hh] + jnp.concatenate([part[0] + part[2], part[1] + part[3]], axis=0)
        if j == 3:
            gq[h] = whole.astype(BF16)
        else:
            gs_z[j] = whole.astype(BF16)
            grad_z.append(push(gs_z.at[j], gq.at[h], dev(dz=(8, 4, 12)[j])))

    finish_grad(0)
    finish_grad(1)
    for copy in feat_window:
        copy.wait_recv()
    own8 = pl.ds(pl.multiple_of(((y % 4) * 32) + l * 8, 8), 8)
    got = feat[own8, :] + wr[0].astype(F32) + wr[1].astype(F32) + wr[2].astype(F32)
    rows8 = hid8[...]
    inverse = inv8[:, 0:1]
    row_dots = jnp.mean(got * gain * rows8, axis=-1, keepdims=True)
    exits = inverse * (gain * got - rows8 * (inverse * inverse * row_dots))
    later = [None] * 4
    later[3] = exits[6:8]
    for k in (2, 1, 0):
        later[k] = exits[2 * k : 2 * k + 2] + later[k + 1]
    ts[...] = later[0].astype(BF16)
    planes = [push(ts, tr.at[i], dev(dx=k)) for i, k in enumerate((1, 2, 3))]
    finish_grad(2)
    finish_grad(3)
    above = jnp.zeros((2, D), F32)
    for i, k in enumerate((1, 2, 3)):
        planes[i].wait_recv()
        above += jnp.where(x + (4 - k) < 4, 1.0, 0.0) * tr[i].astype(F32)
    for k in range(4):
        value = later[k] + above
        sf[k] = value
        cs[k] = value.astype(BF16)
    last = [push(cs.at[(h + k // 4) % 4], cr.at[i], dev(dz=k)) for i, k in enumerate(Z_CLASS)]
    for copy in last:
        copy.wait_recv()
    result = sf[h] + top_ref[...].astype(F32)
    for i in range(3):
        result += cr[i].astype(F32)
    ghid_ref[0] = result.astype(BF16)
    for copy in grad_z:
        copy.wait_recv()
    for k in range(4):
        ghead_ref[k * 128 : k * 128 + 128, :] = gq[k]
    for copy in copies:
        copy.wait_send()


def body(hidden, norm_gain, exit_head, targets, loss_numerators, top_grad):
    vmem = pl.BlockSpec(memory_space=pltpu.VMEM)
    smem = pl.BlockSpec(memory_space=pltpu.SMEM)
    return pl.pallas_call(
        kernel,
        out_shape=(
            jax.ShapeDtypeStruct(exit_head.shape, BF16),
            jax.ShapeDtypeStruct(hidden.shape, BF16),
        ),
        in_specs=[vmem, vmem, vmem, smem, smem, vmem],
        out_specs=(vmem, vmem),
        scratch_shapes=[
            pltpu.VMEM((4, 2, D), BF16),
            pltpu.VMEM((8, D), F32),
            pltpu.VMEM((8, 128), F32),
            pltpu.VMEM((4, 8, D), BF16),
            pltpu.VMEM((256, D), BF16),
            pltpu.VMEM((4, 4, 256, 256), BF16),
            pltpu.VMEM((256, 128), F32),
            pltpu.VMEM((3, 4, 8, 128), F32),
            pltpu.VMEM((256, 128), BF16),
            pltpu.VMEM((2, 128, 128), BF16),
            pltpu.VMEM((128, D), F32),
            pltpu.VMEM((4, 4, 128, 256), F32),
            pltpu.VMEM((2, 32, HALF), BF16),
            pltpu.VMEM((2, 32, HALF), BF16),
            pltpu.VMEM((4, 32, HALF), BF16),
            pltpu.VMEM((4, 32, HALF), BF16),
            pltpu.VMEM((4, 8, D), BF16),
            pltpu.VMEM((3, 8, D), BF16),
            pltpu.VMEM((2, D), BF16),
            pltpu.VMEM((3, 2, D), BF16),
            pltpu.VMEM((4, 2, D), F32),
            pltpu.VMEM((4, 2, D), BF16),
            pltpu.VMEM((3, 2, D), BF16),
            pltpu.VMEM((4, 2, 64, 256), BF16),
            pltpu.VMEM((4, 2, 64, 256), BF16),
            pltpu.VMEM((4, 4, 64, 256), BF16),
            pltpu.VMEM((4, 4, 64, 256), BF16),
            pltpu.VMEM((3, 128, 256), BF16),
            pltpu.VMEM((4, 128, 256), BF16),
            pltpu.SemaphoreType.DMA((COPIES,)),
            pltpu.SemaphoreType.DMA((COPIES,)),
        ],
        compiler_params=pltpu.CompilerParams(
            collective_id=0, has_side_effects=True, vmem_limit_bytes=40 * 1024 * 1024
        ),
        name="exit_head_backward",
    )(hidden, norm_gain.reshape(1, D), exit_head, targets, loss_numerators, top_grad)


def solution(mesh):
    placed = (P("section", "dp", None), P(), P("dp", "section"), P(), P(), P("dp", None))
    return jax.shard_map(
        body,
        mesh=mesh,
        in_specs=placed,
        out_specs=(P("dp", "section"), P("section", "dp", None)),
        check_vma=False,
    )
```

time: 1180 us -> 111 us (0.09)
  the two profiles are of different devices: /device:TPU:6 before, /device:TPU:40 now
where the time goes in v1:
time: 111 us
  Pallas kernels  105 us (95%)
  local copies, waits for them, and re-layouts  5.07 us (5%)
    pallas_call x1, Pallas kernels, body(): pl.pallas_call(kernel, out_shape=(jax.ShapeDtypeStruct(exit_head.shape, B...  105 us
    unnamed x14, local copies, waits for them, and re-layouts  5.07 us

profile of v1, /device:TPU:40, one launch (start us, length us, event | category | flops | bytes accessed | tf_op | source)
XLA Modules:
  0.0 110.5 jit_solution(1403130692296774593)
XLA Ops:
  0.6 0.0 copy-start.5
  0.6 0.0 copy-start.4
  0.7 0.6 copy-done.5
  1.3 0.0 copy-done.4
  1.3 0.0 copy-start
  1.3 0.9 copy-done
  2.3 0.0 copy-start.1
  2.3 0.7 copy-done.1
  3.0 0.0 copy-start.2
  3.0 0.7 copy-done.2
  3.7 0.0 copy-start.3
  3.7 0.7 copy-done.3
  4.4 104.8 %exit_head_backward.1 = (bf16[512,256]{1,0:T(8,128)(2,1)S(1)}, bf16[1,2,4096]{2,1,0:T(2,128)(2,1)S(1)}) custom-call(bf16[1,2,4096]{2,1,0:T(2,128)(2,1)S(1)} %copy-done.1, f32[1,4096]{1,0:T(1,128)S(1)} %bitcast.1, bf16[512,256]{1,0:T(8,128)(2,1)S(1)} %copy-done, s32[64]{0:T(128)S(1)} %copy-done.4, s32[16]{0:T(128)S(1)} %copy-done.5, bf16[2,4096]{1,0:T(2,128)(2,1)S(1)} %copy-done.3), custom_call_target="tpu_custom_call" | custom-call | tf_op jit(solution)/shard_map/exit_head_backward/pallas_call | solution.py:316
  109.2 0.7 copy.10
  109.9 0.6 copy.11
Async XLA Ops:
  0.6 0.7 copy-start.5
  0.6 0.7 copy-start.4
  1.3 0.9 copy-start
  2.3 0.7 copy-start.1
  3.0 0.7 copy-start.2
  3.7 0.7 copy-start.3

commit v2 on v0

v2 whole, which is shorter than its diff:
```python
import functools

import jax
import jax.numpy as jnp
from jax import lax
from jax.experimental import pallas as pl
from jax.experimental.pallas import tpu as pltpu
from jax.sharding import PartitionSpec as P

MESH = pl.DeviceIdType.MESH
EXIT_DENOM = 16
EPSILON = 1e-05
F32 = jnp.float32
BF16 = jnp.bfloat16
D = 4096
SENDS = 18
RECVS = 36
LOCALS = 6
Z_WINDOW = (1, 15, 2)
Z_CLASS = (8, 4, 12)
RING = (1, 3, 2)


def dot(a, b, contract):
    return lax.dot_general(a, b, (contract, ((), ())), preferred_element_type=F32)


def kernel(
    hidden_ref, gain_ref, head_ref, targets_ref, nums_ref, top_ref,
    ghead_ref, ghid_ref,
    hid, gain_v, top_v, hid8, inv8, pieces, norm, heads, logits, stats_1, stats_2, dlog_t, dlog_2,
    coef, hs, hr, hx, feat, fs, fr, wo, ws, wr, ts, tr, sf, cs, cr, grad, gs, gr, gs_z, gq,
    targets_s, nums_s, send_sem, recv_sem, local_sem,
):
    sec, dp = lax.axis_index("section"), lax.axis_index("dp")
    x, h = sec // 4, sec % 4
    l, y, c = dp // 8, (dp // 2) % 4, dp % 2
    z = 4 * h + l

    def dev(dx=0, dy=0, dz=0, flip=False):
        nx, ny, nz = (x + dx) % 4, (y + dy) % 4, (z + dz) % 16
        nc = 1 - c if flip else c
        return {"section": nx * 4 + nz // 4, "dp": (nz % 4) * 8 + ny * 2 + nc}

    counts = {"send": 0, "recv": 0}
    sent = []

    def new_recv():
        counts["recv"] += 1
        return recv_sem.at[counts["recv"] - 1]

    def new_send(total):
        counts["send"] += 1
        sem = send_sem.at[counts["send"] - 1]
        sent.append((sem, total))
        return sem

    def push(src, dst, where, s_sem, r_sem):
        pltpu.make_async_remote_copy(
            src_ref=src, dst_ref=dst, send_sem=s_sem, recv_sem=r_sem,
            device_id=where, device_id_type=MESH,
        ).start()

    def wait(sem, total):
        pltpu.make_async_copy(total, total, sem).wait()

    mine = pl.ds(pl.multiple_of(c * 128, 128), 128)
    other = pl.ds(pl.multiple_of((1 - c) * 128, 128), 128)

    def quarter(hh):
        return head_ref.at[pl.ds(pl.multiple_of(hh * 128, 128), 128)]

    locals_ = [
        pltpu.make_async_copy(src, dst, local_sem.at[i])
        for i, (src, dst) in enumerate((
            (hidden_ref.at[0], hid.at[h]),
            (quarter(h), heads.at[x, h, mine]),
            (gain_ref, gain_v),
            (targets_ref, targets_s),
            (nums_ref, nums_s),
            (top_ref, top_v),
        ))
    ]
    for copy in locals_:
        copy.start()

    barrier = pltpu.get_barrier_semaphore()
    near_z = (1, 15, 2, 14)
    partners = [dev(dz=k) for k in Z_CLASS + near_z] + [dev(dx=k) for k in RING] + [dev(flip=True)]
    partners += [dev(dy=k) for k in RING] + [dev(dy=i, dz=k) for i in RING for k in near_z]
    for where in partners:
        pl.semaphore_signal(barrier, inc=1, device_id=where, device_id_type=MESH)
    pl.semaphore_wait(barrier, len(partners))

    hid_s, hid_r = new_send(hid.at[0:3]), new_recv()
    for k in Z_CLASS:
        push(hidden_ref.at[0], hid.at[h], dev(dz=k), hid_s, hid_r)
    headz_s, headz_r = new_send(heads.at[0, 0:3, 0:128]), [new_recv() for _ in Z_CLASS]

    def transpose(which):
        for i in which:
            k = Z_CLASS[i]
            push(quarter((h + k // 4) % 4), heads.at[x, h, mine], dev(dz=k), headz_s, headz_r[i])

    transpose((0,))
    headx_s, headx_r = new_send(heads.at[0:3, :, 0:128]), [new_recv() for _ in range(4)]

    def spread(hh, sem):
        block = heads.at[x, hh, mine]
        for k in RING:
            push(block, block, dev(dx=k), headx_s, sem)

    locals_[1].wait()
    spread(h, headx_r[0])
    for i in (0, 2, 3, 4, 5):
        locals_[i].wait()

    lane = lax.broadcasted_iota(jnp.int32, (1, 128), 1)
    lane_y, lane_l, lane_h, lane_r = lane // 32, (lane // 8) % 4, (lane // 2) % 4, lane % 2
    row_of = lane_l * 16 + lane_y * 4 + lane_r
    target = jnp.zeros((1, 128), jnp.int32)
    for k in range(64):
        if (k // 2) % 2 == 0:
            target = jnp.where(row_of == k, targets_s[k + 2 * c], target)
    weight = jnp.zeros((1, 128), F32)
    for k in range(4):
        weight = jnp.where(lane_h == k, nums_s[x * 4 + k].astype(F32) / EXIT_DENOM, weight)

    slot = lax.broadcasted_iota(jnp.int32, (32, 1), 0)
    target_col = jnp.zeros((32, 1), jnp.int32)
    for k in range(32):
        target_col = jnp.where(slot == k, targets_s[(k // 2) % 4 * 16 + k // 8 * 4 + k % 2 + 2 * c], target_col)
    first_id = 1024 * (l * 4 + y) + 128 * h
    lane_id = lax.broadcasted_iota(jnp.int32, (1, 256), 1)
    picks = jnp.where(first_id + lane_id + 384 * (lane_id // 128) == target_col, 1.0, 0.0).astype(BF16)

    wait(hid_r, hid.at[0:3])
    gain = gain_v[...]
    rows8 = jnp.concatenate([hid[k].astype(F32) for k in range(4)], axis=0)
    inverse = lax.rsqrt(jnp.mean(rows8 * rows8, axis=-1, keepdims=True) + EPSILON)
    pieces[y, l] = (rows8 * inverse * gain).astype(BF16)
    window_s, window_r = new_send(pieces.at[0, 0:3]), [new_recv() for _ in Z_WINDOW]
    ring_s, ring_r = new_send(pieces.at[0:3]), [new_recv() for _ in RING]
    own = pieces.at[y, l]
    for k, sem in zip((1, 15), window_r):
        push(own, own, dev(dz=k), window_s, sem)
    for k, cols in ((2, pl.ds(0, D // 2)), (14, pl.ds(D // 2, D // 2))):
        part = pieces.at[y, l, :, cols]
        push(part, part, dev(dz=k), window_s, window_r[2])
    transpose((1, 2))
    for k, sem in zip(RING, ring_r):
        push(own, own, dev(dy=k), ring_s, sem)
    hid8[...] = rows8
    inv8[...] = jnp.broadcast_to(inverse, (8, 128))

    for k, sem in zip(Z_WINDOW, window_r):
        piece = pieces.at[y, (l - k) % 4]
        wait(sem, piece)
        for kk, ring in zip(RING, ring_r):
            push(piece, piece, dev(dy=kk), ring_s, ring)

    order = [h] + [(h - k // 4) % 4 for k in Z_CLASS[1:] + Z_CLASS[:1]]
    for j in (1, 2, 3):
        wait(headz_r[j % 3], heads.at[x, order[j], mine])
        spread(order[j], headx_r[j])

    def assemble(yy):
        for half in range(2):
            both = jnp.concatenate([pieces[yy, 2 * half + k].astype(F32) for k in range(2)], axis=0)
            rows = pl.ds(pl.multiple_of(c * 128 + yy * 32 + half * 16, 16), 16)
            norm[rows, :] = both.astype(BF16)

    assemble(y)
    for k, sem in zip(RING, ring_r):
        wait(sem, pieces.at[0])
        assemble((y - k) % 4)
    norm_s, norm_r = new_send(norm.at[mine]), new_recv()
    push(norm.at[mine], norm.at[mine], dev(flip=True), norm_s, norm_r)

    core_s, core_r = new_send(heads.at[:, :, 0:128]), [new_recv() for _ in range(4)]
    logits[...] = jnp.zeros((256, 128), F32)
    for j, hh in enumerate(order):
        wait(headx_r[j], heads.at[0:3, hh, mine])
        block = heads.at[:, hh, mine]
        push(block, block, dev(flip=True), core_s, core_r[j])
        wait(core_r[j], block)
        part = jnp.zeros((256, 128), F32)
        for k in range(4):
            cols = pl.ds(pl.multiple_of((k * 4 + hh) * 256, 256), 256)
            part += dot(heads[k, hh], norm[mine, cols], ((1,), (1,)))
        logits[...] += part
    values = logits[...]
    row = lax.broadcasted_iota(jnp.int32, (256, 128), 0)
    at_target = first_id + row + 384 * (row // 128) == target
    first_peak = jnp.max(values, axis=0, keepdims=True)
    expo = jnp.exp(values - first_peak)
    others = jnp.where(at_target, 0.0, expo)
    own_stats = jnp.concatenate(
        [
            first_peak,
            jnp.sum(others, axis=0, keepdims=True),
            jnp.sum(jnp.where(at_target, expo, 0.0), axis=0, keepdims=True),
            jnp.zeros((5, 128), F32),
        ],
        axis=0,
    )

    def send_stats(stats, mine_now, peers):
        n = len(peers)
        s_sem, r_sem = new_send(stats.at[0:n]), new_recv()
        stats[n] = mine_now
        for i, where in enumerate(peers):
            push(stats.at[n], stats.at[i], where, s_sem, r_sem)
        return r_sem

    def combine(stats, r_sem, n):
        wait(r_sem, stats.at[0:n])
        parts = [stats[i] for i in range(n + 1)]
        top = functools.reduce(jnp.maximum, [part[0:1] for part in parts])
        sums = sum(part[1:3] * jnp.exp(part[0:1] - top) for part in parts)
        return jnp.concatenate([top, sums, jnp.zeros((5, 128), F32)], axis=0)

    peers = [dev(dy=i, dz=k) for k in Z_WINDOW + (0,) for i in RING + (0,)][:-1]
    stats_r = send_stats(stats_1, own_stats, peers)

    pick_s, pick_r = new_send(hr), new_recv()
    for k in range(4):
        part = dot(picks, heads[x, k], ((1,), (0,)))
        for yy in range(4):
            hs[yy, :, 256 * k : 256 * k + 256] = part[8 * yy : 8 * yy + 8].astype(BF16)
    for i, k in enumerate(RING):
        push(hs.at[(y + k) % 4], hr.at[i], dev(dy=k), pick_s, pick_r)

    others_n = others.T.astype(BF16)
    feat_s, feat_r = new_send(fr), [new_recv() for _ in range(4)]
    for q in range(4):
        for k in range(4):
            part = dot(others_n, heads[q, k], ((1,), (0,)))
            for yy in range(4):
                rows = part[32 * yy : 32 * yy + 32]
                feat[q, yy, :, 256 * k : 256 * k + 256] = rows
                fs[q, yy, :, 256 * k : 256 * k + 256] = rows.astype(BF16)
        for i, k in enumerate(RING):
            push(fs.at[q, (y + k) % 4], fr.at[q, i], dev(dy=k), feat_s, feat_r[q])

    summed_stats = combine(stats_1, stats_r, 15)
    stats_r = send_stats(stats_2, summed_stats, [dev(dz=k) for k in Z_CLASS])
    wait(pick_r, hr)
    hx[x] = (hs[y].astype(F32) + hr[0].astype(F32) + hr[1].astype(F32) + hr[2].astype(F32)).astype(BF16)
    pickx_s, pickx_r = new_send(hx.at[0:3]), new_recv()
    for k in RING:
        push(hx.at[x], hx.at[x], dev(dx=k), pickx_s, pickx_r)
    summed_stats = combine(stats_2, stats_r, 3)
    peak = summed_stats[0:1]
    total = summed_stats[1:2] + summed_stats[2:3]
    scale = weight / total

    dlog = expo * (scale * jnp.exp(first_peak - peak)) - jnp.where(at_target, weight, 0.0)
    dlog_t[...] = dlog.astype(BF16)
    dlog_s, dlog_r = new_send(dlog_2.at[0]), new_recv()
    push(dlog_t.at[other], dlog_2.at[c], dev(flip=True), dlog_s, dlog_r)
    dlog_2[c] = dlog_t[mine, :]
    coef[...] = jnp.concatenate(
        [scale * jnp.exp(stats_1[i][0:1] - peak) for i in (12, 13, 14, 15)]
        + [scale * summed_stats[1:2], jnp.zeros((123, 128), F32)],
        axis=0,
    ).T
    factors = coef[pl.ds(pl.multiple_of(32 * y, 32), 32), :]

    wait(dlog_r, dlog_2.at[0])
    wait(norm_r, norm.at[other])
    dlog_all = jnp.concatenate([dlog_2[0], dlog_2[1]], axis=1)
    grad_order = [(h + k // 4) % 4 for k in Z_CLASS] + [h]
    grad_s, grad_r = new_send(gr), [new_recv() for _ in range(4)]

    def start_grad(j):
        for k in range(4):
            cols = pl.ds(pl.multiple_of((k * 4 + grad_order[j]) * 256, 256), 256)
            part = dot(dlog_all, norm[:, cols], ((1,), (0,)))
            grad[j, k] = part
            gs[j, k] = part.astype(BF16)
        for i, k in enumerate(RING):
            push(gs.at[j, (x + k) % 4], gr.at[j, i], dev(dx=k), grad_s, grad_r[j])

    swin_s, swin_r = new_send(wr), new_recv()
    gradz_s, gradz_r = new_send(gs_z), new_recv()

    def finish_feat(q):
        wait(feat_r[q], fr.at[q])
        summed = factors[:, 3:4] * feat[q, y]
        for i in range(3):
            summed += factors[:, i : i + 1] * fr[q, i].astype(F32)
        rows = hx[q].astype(F32)
        rows = jnp.concatenate([rows[2 * (k // 4) : 2 * (k // 4) + 2] for k in range(16)], axis=0)
        summed -= factors[:, 4:5] * rows
        for k in range(4):
            wo[q, k] = summed[8 * k : 8 * k + 8]
            ws[q, k] = summed[8 * k : 8 * k + 8].astype(BF16)
        for i, k in enumerate((1, 15, 2 if q < 2 else 14)):
            push(ws.at[q, (l + k) % 4], wr.at[q, i], dev(dz=k), swin_s, swin_r)

    def finish_grad(j):
        wait(grad_r[j], gr.at[j])
        whole = grad[j, x] + gr[j, 0].astype(F32) + gr[j, 1].astype(F32) + gr[j, 2].astype(F32)
        if j == 3:
            gq[h] = whole.astype(BF16)
        else:
            gs_z[j] = whole.astype(BF16)
            push(gs_z.at[j], gq.at[h], dev(dz=Z_CLASS[j]), gradz_s, gradz_r)

    start_grad(0)
    wait(pickx_r, hx.at[0:3])
    finish_feat(0)
    finish_feat(1)
    start_grad(1)
    finish_feat(2)
    finish_feat(3)
    start_grad(2)
    start_grad(3)
    for j in range(4):
        finish_grad(j)

    wait(swin_r, wr)
    got = jnp.concatenate(
        [wo[q, l] + wr[q, 0].astype(F32) + wr[q, 1].astype(F32) + wr[q, 2].astype(F32) for q in range(4)],
        axis=1,
    )
    rows8 = hid8[...]
    inverse = inv8[:, 0:1]
    row_dots = jnp.mean(got * gain * rows8, axis=-1, keepdims=True)
    exits = inverse * (gain * got - rows8 * (inverse * inverse * row_dots))
    later = [None] * 4
    later[3] = exits[6:8]
    for k in (2, 1, 0):
        later[k] = exits[2 * k : 2 * k + 2] + later[k + 1]
    ts[...] = later[0].astype(BF16)
    plane_s, plane_r = new_send(tr), new_recv()
    for i, k in enumerate(RING):
        push(ts, tr.at[i], dev(dx=k), plane_s, plane_r)
    wait(plane_r, tr)
    above = jnp.zeros((2, D), F32)
    for i, k in enumerate(RING):
        above += jnp.where(x + (4 - k) < 4, 1.0, 0.0) * tr[i].astype(F32)
    for k in range(4):
        value = later[k] + above
        sf[k] = value
        cs[k] = value.astype(BF16)
    class_s, class_r = new_send(cr), new_recv()
    for i, k in enumerate(Z_CLASS):
        push(cs.at[(h + k // 4) % 4], cr.at[i], dev(dz=k), class_s, class_r)
    wait(class_r, cr)
    result = sf[h] + top_v[...].astype(F32)
    for i in range(3):
        result += cr[i].astype(F32)
    ghid_ref[0] = result.astype(BF16)
    wait(gradz_r, gq.at[0:3])
    for k in range(4):
        ghead_ref[k * 128 : k * 128 + 128, :] = gq[k]
    assert counts == {"send": SENDS, "recv": RECVS}
    for sem, ref in sent:
        wait(sem, ref)


def body(hidden, norm_gain, exit_head, targets, loss_numerators, top_grad):
    vmem = pl.BlockSpec(memory_space=pltpu.VMEM)
    where_it_is = pl.BlockSpec(memory_space=pl.ANY)
    return pl.pallas_call(
        kernel,
        out_shape=(
            jax.ShapeDtypeStruct(exit_head.shape, BF16),
            jax.ShapeDtypeStruct(hidden.shape, BF16),
        ),
        in_specs=[where_it_is] * 6,
        out_specs=(vmem, vmem),
        scratch_shapes=[
            pltpu.VMEM((4, 2, D), BF16),
            pltpu.VMEM((1, D), F32),
            pltpu.VMEM((2, D), BF16),
            pltpu.VMEM((8, D), F32),
            pltpu.VMEM((8, 128), F32),
            pltpu.VMEM((4, 4, 8, D), BF16),
            pltpu.VMEM((256, D), BF16),
            pltpu.VMEM((4, 4, 256, 256), BF16),
            pltpu.VMEM((256, 128), F32),
            pltpu.VMEM((16, 8, 128), F32),
            pltpu.VMEM((4, 8, 128), F32),
            pltpu.VMEM((256, 128), BF16),
            pltpu.VMEM((2, 128, 128), BF16),
            pltpu.VMEM((128, 128), F32),
            pltpu.VMEM((4, 8, 1024), BF16),
            pltpu.VMEM((3, 8, 1024), BF16),
            pltpu.VMEM((4, 8, 1024), BF16),
            pltpu.VMEM((4, 4, 32, 1024), F32),
            pltpu.VMEM((4, 4, 32, 1024), BF16),
            pltpu.VMEM((4, 3, 32, 1024), BF16),
            pltpu.VMEM((4, 4, 8, 1024), F32),
            pltpu.VMEM((4, 4, 8, 1024), BF16),
            pltpu.VMEM((4, 3, 8, 1024), BF16),
            pltpu.VMEM((2, D), BF16),
            pltpu.VMEM((3, 2, D), BF16),
            pltpu.VMEM((4, 2, D), F32),
            pltpu.VMEM((4, 2, D), BF16),
            pltpu.VMEM((3, 2, D), BF16),
            pltpu.VMEM((4, 4, 128, 256), F32),
            pltpu.VMEM((4, 4, 128, 256), BF16),
            pltpu.VMEM((4, 3, 128, 256), BF16),
            pltpu.VMEM((3, 128, 256), BF16),
            pltpu.VMEM((4, 128, 256), BF16),
            pltpu.SMEM((64,), jnp.int32),
            pltpu.SMEM((16,), jnp.int32),
            pltpu.SemaphoreType.DMA((SENDS,)),
            pltpu.SemaphoreType.DMA((RECVS,)),
            pltpu.SemaphoreType.DMA((LOCALS,)),
        ],
        compiler_params=pltpu.CompilerParams(
            collective_id=0, has_side_effects=True, vmem_limit_bytes=60 * 1024 * 1024
        ),
        name="exit_head_backward",
    )(hidden, norm_gain.reshape(1, D), exit_head, targets, loss_numerators, top_grad)


def solution(mesh):
    placed = (P("section", "dp", None), P(), P("dp", "section"), P(), P(), P("dp", None))
    return jax.shard_map(
        body,
        mesh=mesh,
        in_specs=placed,
        out_specs=(P("dp", "section"), P("section", "dp", None)),
        check_vma=False,
    )
```

time: 1180 us -> 90.4 us (0.08)
  waiting for transfers between devices: 778 us -> 0 us
  blocking collectives: 201 us -> 0 us
  starting transfers between devices: 130 us -> 0 us
  Pallas kernels: 0 us -> 87.3 us
  other arithmetic: 34 us -> 0 us
  local copies, waits for them, and re-layouts: 16.6 us -> 2.28 us
  between operations: 13.8 us -> 0.65 us
    psum x2 -> x0, waiting for transfers between devices: 412 us -> none  [one_block(): logits = lax.psum(partial_logits, 'section')]
    reduce_scatter x2 -> x0, waiting for transfers between devices: 287 us -> none  [one_block(): lax.psum_scatter(feat_back, 'dp', scatter_dimension=1, tiled=True)]
    all_gather x5 -> x0, blocking collectives: 201 us -> none  [the longest x4 157 us: joined(): pieces = jax.tree.map(lambda part: lax.all_gather(part, axis), value)]
    ppermute x15 -> x0, starting transfers between devices: 99.5 us -> none  [passed_along(): return lax.ppermute(block, axis, route)]
    pallas_call x0 -> x1, Pallas kernels: none -> 87.3 us  [body(): pl.pallas_call(kernel, out_shape=(jax.ShapeDtypeStruct(exit_head.shape, B...]
    ppermute x15 -> x0, waiting for transfers between devices: 54.4 us -> none  [passed_along(): return lax.ppermute(block, axis, route)]
    all_to_all x2 -> x0, starting transfers between devices: 30.7 us -> none  [the longest x1 18 us: body(): lax.all_to_all(normed, 'section', split_axis=2, concat_axis=0, tiled=True)]
    all_to_all x2 -> x0, waiting for transfers between devices: 24.6 us -> none  [the longest x1 12.5 us: body(): lax.all_to_all(normed, 'section', split_axis=2, concat_axis=0, tiled=True)]
  transfers between devices with their start and end apart: 21 -> 0, of which waited for: 21 -> 0; matrix products, arithmetic and copies ran while one was open for 0% -> 0% of each run, Pallas kernels for 0% -> 0%
where the time goes in v2:
time: 90.4 us; the launch traced here: 90.2 us
  Pallas kernels  87.3 us (97%)
  local copies, waits for them, and re-layouts  2.28 us (3%)
    pallas_call x1, Pallas kernels, body(): pl.pallas_call(kernel, out_shape=(jax.ShapeDtypeStruct(exit_head.shape, B...  87.3 us
    unnamed x4, local copies, waits for them, and re-layouts  2.28 us

profile of v2, /device:TPU:6, one launch (start us, length us, event | category | flops | bytes accessed | tf_op | source)
XLA Modules:
  0.0 90.2 jit_solution(3660279425295059936)
XLA Ops:
  0.6 87.3 %exit_head_backward.1 = (bf16[512,256]{1,0:T(8,128)(2,1)}, bf16[1,2,4096]{2,1,0:T(2,128)(2,1)}) custom-call(bf16[1,2,4096]{2,1,0:T(2,128)(2,1)} %hidden_ref.1, f32[1,4096]{1,0:T(1,128)} %bitcast.1, bf16[512,256]{1,0:T(8,128)(2,1)} %head_ref.1, s32[64]{0:T(128)} %targets_ref.1, s32[16]{0:T(128)} %nums_ref.1, bf16[2,4096]{1,0:T(2,128)(2,1)} %top_ref.1), custom_call_target="tpu_custom_call" | custom-call | tf_op jit(solution)/shard_map/exit_head_backward/pallas_call | solution.py:367
  87.9 0.0 copy-start
  87.9 1.7 %copy.10 = bf16[512,256]{1,0:T(8,128)(2,1)} copy(bf16[512,256]{1,0:T(8,128)(2,1)} %get-tuple-element.4) | data formatting | bytes 524288
  89.6 0.0 copy-done
  89.6 0.6 copy.11
Async XLA Ops:
  87.9 1.7 %copy-start = (bf16[1,2,4096]{2,1,0:T(2,128)(2,1)S(1)}, bf16[1,2,4096]{2,1,0:T(2,128)(2,1)}, u32[]{:S(2)}) copy-start(bf16[1,2,4096]{2,1,0:T(2,128)(2,1)} %get-tuple-element.5) | copy-start | bytes 49156

commit v3 on v2

--- a/solution.py
+++ b/solution.py
@@ -13,8 +13,8 @@
 F32 = jnp.float32
 BF16 = jnp.bfloat16
 D = 4096
-SENDS = 18
-RECVS = 36
+SENDS = 24
+RECVS = 55
 LOCALS = 6
 Z_WINDOW = (1, 15, 2)
 Z_CLASS = (8, 4, 12)
@@ -28,8 +28,8 @@
 def kernel(
     hidden_ref, gain_ref, head_ref, targets_ref, nums_ref, top_ref,
     ghead_ref, ghid_ref,
-    hid, gain_v, top_v, hid8, inv8, pieces, norm, heads, logits, stats_1, stats_2, dlog_t, dlog_2,
-    coef, hs, hr, hx, feat, fs, fr, wo, ws, wr, ts, tr, sf, cs, cr, grad, gs, gr, gs_z, gq,
+    raw, gain_v, top_v, norm, heads, logits, stats_1, stats_2, expo_t, expo_all, own_all, plane_all, norm_all,
+    coef, hs, hr, hx, feat, fs, fr, wo, ws, wr, ts, tr, sf, cs, cr,
     targets_s, nums_s, send_sem, recv_sem, local_sem,
 ):
     sec, dp = lax.axis_index("section"), lax.axis_index("dp")
@@ -73,7 +73,7 @@
     locals_ = [
         pltpu.make_async_copy(src, dst, local_sem.at[i])
         for i, (src, dst) in enumerate((
-            (hidden_ref.at[0], hid.at[h]),
+            (hidden_ref.at[0], raw.at[y, l, h]),
             (quarter(h), heads.at[x, h, mine]),
             (gain_ref, gain_v),
             (targets_ref, targets_s),
@@ -92,9 +92,27 @@
         pl.semaphore_signal(barrier, inc=1, device_id=where, device_id_type=MESH)
     pl.semaphore_wait(barrier, len(partners))
 
-    hid_s, hid_r = new_send(hid.at[0:3]), new_recv()
-    for k in Z_CLASS:
-        push(hidden_ref.at[0], hid.at[h], dev(dz=k), hid_s, hid_r)
+    class_pieces = [new_recv() for _ in Z_CLASS]
+    window_pieces = [[new_recv() for _ in range(3)] for _ in range(4)]
+    ring_pieces = [new_recv() for _ in RING]
+    classp_s, windowp_s, ringp_s = new_send(raw.at[0, 0, 0:3]), new_send(raw.at[0, 0:3]), new_send(raw.at[0:3])
+    cols_a, cols_b = pl.ds(0, D // 2), pl.ds(D // 2, D // 2)
+    mine_now = hidden_ref.at[0]
+    for k, sem in zip(Z_CLASS, class_pieces):
+        push(mine_now, raw.at[y, l, h], dev(dz=k), classp_s, sem)
+
+    def to_window(src, slot, sems):
+        push(src, slot, dev(dz=1), windowp_s, sems[0])
+        push(src, slot, dev(dz=15), windowp_s, sems[1])
+        push(src.at[:, cols_a], slot.at[:, cols_a], dev(dz=2), windowp_s, sems[2])
+        push(src.at[:, cols_b], slot.at[:, cols_b], dev(dz=14), windowp_s, sems[2])
+
+    def to_ring(src, slot):
+        for k, sem in zip(RING, ring_pieces):
+            push(src, slot, dev(dy=k), ringp_s, sem)
+
+    to_window(mine_now, raw.at[y, l, h], window_pieces[0])
+    to_ring(mine_now, raw.at[y, l, h])
     headz_s, headz_r = new_send(heads.at[0, 0:3, 0:128]), [new_recv() for _ in Z_CLASS]
 
     def transpose(which):
@@ -102,7 +120,7 @@
             k = Z_CLASS[i]
             push(quarter((h + k // 4) % 4), heads.at[x, h, mine], dev(dz=k), headz_s, headz_r[i])
 
-    transpose((0,))
+    transpose((1, 2))
     headx_s, headx_r = new_send(heads.at[0:3, :, 0:128]), [new_recv() for _ in range(4)]
 
     def spread(hh, sem):
@@ -118,14 +136,21 @@
     lane = lax.broadcasted_iota(jnp.int32, (1, 128), 1)
     lane_y, lane_l, lane_h, lane_r = lane // 32, (lane // 8) % 4, (lane // 2) % 4, lane % 2
     row_of = lane_l * 16 + lane_y * 4 + lane_r
-    target = jnp.zeros((1, 128), jnp.int32)
-    for k in range(64):
-        if (k // 2) % 2 == 0:
-            target = jnp.where(row_of == k, targets_s[k + 2 * c], target)
-    weight = jnp.zeros((1, 128), F32)
-    for k in range(4):
-        weight = jnp.where(lane_h == k, nums_s[x * 4 + k].astype(F32) / EXIT_DENOM, weight)
-
+    def lane_targets(core):
+        found = jnp.zeros((1, 128), jnp.int32)
+        for k in range(64):
+            if (k // 2) % 2 == 0:
+                found = jnp.where(row_of == k, targets_s[k + 2 * core], found)
+        return found
+
+    def lane_weights(plane):
+        found = jnp.zeros((1, 128), F32)
+        for k in range(4):
+            found = jnp.where(lane_h == k, nums_s[plane * 4 + k].astype(F32) / EXIT_DENOM, found)
+        return found
+
+    target, weight = lane_targets(c), lane_weights(x)
+    both_targets = jnp.concatenate([lane_targets(0), lane_targets(1)], axis=1)
     slot = lax.broadcasted_iota(jnp.int32, (32, 1), 0)
     target_col = jnp.zeros((32, 1), jnp.int32)
     for k in range(32):
@@ -134,48 +159,65 @@
     lane_id = lax.broadcasted_iota(jnp.int32, (1, 256), 1)
     picks = jnp.where(first_id + lane_id + 384 * (lane_id // 128) == target_col, 1.0, 0.0).astype(BF16)
 
-    wait(hid_r, hid.at[0:3])
-    gain = gain_v[...]
-    rows8 = jnp.concatenate([hid[k].astype(F32) for k in range(4)], axis=0)
-    inverse = lax.rsqrt(jnp.mean(rows8 * rows8, axis=-1, keepdims=True) + EPSILON)
-    pieces[y, l] = (rows8 * inverse * gain).astype(BF16)
-    window_s, window_r = new_send(pieces.at[0, 0:3]), [new_recv() for _ in Z_WINDOW]
-    ring_s, ring_r = new_send(pieces.at[0:3]), [new_recv() for _ in RING]
-    own = pieces.at[y, l]
-    for k, sem in zip((1, 15), window_r):
-        push(own, own, dev(dz=k), window_s, sem)
-    for k, cols in ((2, pl.ds(0, D // 2)), (14, pl.ds(D // 2, D // 2))):
-        part = pieces.at[y, l, :, cols]
-        push(part, part, dev(dz=k), window_s, window_r[2])
-    transpose((1, 2))
-    for k, sem in zip(RING, ring_r):
-        push(own, own, dev(dy=k), ring_s, sem)
-    hid8[...] = rows8
-    inv8[...] = jnp.broadcast_to(inverse, (8, 128))
-
-    for k, sem in zip(Z_WINDOW, window_r):
-        piece = pieces.at[y, (l - k) % 4]
-        wait(sem, piece)
-        for kk, ring in zip(RING, ring_r):
-            push(piece, piece, dev(dy=kk), ring_s, ring)
+    def from_window(i, steps):
+        for n, k in enumerate((1, 15)):
+            slot = raw.at[y, (l - k) % 4, (((z - k) % 16) // 4 - steps) % 4]
+            wait(window_pieces[i][n], slot)
+            to_ring(slot, slot)
+
+    def from_far(i, steps):
+        wait(window_pieces[i][2], raw.at[0, 0, 0])
+        for k, cols in ((2, cols_a), (14, cols_b)):
+            slot = raw.at[y, (l + 2) % 4, (((z - k) % 16) // 4 - steps) % 4, :, cols]
+            for kk, sem in zip(RING, ring_pieces):
+                push(slot, slot, dev(dy=kk), ringp_s, sem)
+
+    def from_class(i, steps):
+        slot = raw.at[y, l, (h - steps) % 4]
+        wait(class_pieces[i], slot)
+        to_window(slot, slot, window_pieces[i + 1])
+        to_ring(slot, slot)
 
     order = [h] + [(h - k // 4) % 4 for k in Z_CLASS[1:] + Z_CLASS[:1]]
-    for j in (1, 2, 3):
+
+    def from_head(j):
         wait(headz_r[j % 3], heads.at[x, order[j], mine])
         spread(order[j], headx_r[j])
 
+    from_window(0, 0)
+    from_far(0, 0)
+    from_class(1, 1)
+    from_class(2, 3)
+    transpose((0,))
+    from_class(0, 2)
+    from_head(1)
+    from_head(2)
+    from_window(2, 1)
+    from_window(3, 3)
+    from_far(2, 1)
+    from_far(3, 3)
+    from_window(1, 2)
+    from_far(1, 2)
+    gain = gain_v[...]
+
+    def rows_of(yy, ll):
+        rows = jnp.concatenate([raw[yy, ll, k].astype(F32) for k in range(4)], axis=0)
+        return rows, lax.rsqrt(jnp.mean(rows * rows, axis=-1, keepdims=True) + EPSILON)
+
     def assemble(yy):
         for half in range(2):
-            both = jnp.concatenate([pieces[yy, 2 * half + k].astype(F32) for k in range(2)], axis=0)
-            rows = pl.ds(pl.multiple_of(c * 128 + yy * 32 + half * 16, 16), 16)
-            norm[rows, :] = both.astype(BF16)
+            both = []
+            for ll in (2 * half, 2 * half + 1):
+                rows, inverse = rows_of(yy, ll)
+                both.append(rows * inverse * gain)
+            at = pl.ds(pl.multiple_of(yy * 32 + half * 16, 16), 16)
+            norm[at, :] = jnp.concatenate(both, axis=0).astype(BF16)
 
     assemble(y)
-    for k, sem in zip(RING, ring_r):
-        wait(sem, pieces.at[0])
+    from_head(3)
+    for k, sem in zip(RING, ring_pieces):
+        wait(sem, raw.at[0])
         assemble((y - k) % 4)
-    norm_s, norm_r = new_send(norm.at[mine]), new_recv()
-    push(norm.at[mine], norm.at[mine], dev(flip=True), norm_s, norm_r)
 
     core_s, core_r = new_send(heads.at[:, :, 0:128]), [new_recv() for _ in range(4)]
     logits[...] = jnp.zeros((256, 128), F32)
@@ -187,7 +229,7 @@
         part = jnp.zeros((256, 128), F32)
         for k in range(4):
             cols = pl.ds(pl.multiple_of((k * 4 + hh) * 256, 256), 256)
-            part += dot(heads[k, hh], norm[mine, cols], ((1,), (1,)))
+            part += dot(heads[k, hh], norm[:, cols], ((1,), (1,)))
         logits[...] += part
     values = logits[...]
     row = lax.broadcasted_iota(jnp.int32, (256, 128), 0)
@@ -223,6 +265,19 @@
     peers = [dev(dy=i, dz=k) for k in Z_WINDOW + (0,) for i in RING + (0,)][:-1]
     stats_r = send_stats(stats_1, own_stats, peers)
 
+    expo_t[...] = others.astype(BF16)
+    core_e_s, core_e_r = new_send(expo_all.at[0, 0, 0]), new_recv()
+    push(expo_t.at[other], expo_all.at[x, h, c], dev(flip=True), core_e_s, core_e_r)
+    expo_all[x, h, c] = expo_t[mine, :]
+    core_o_s, core_o_r = new_send(own_all.at[0, 0, 0]), new_recv()
+    own_all[x, h, c] = own_stats
+    push(own_all.at[x, h, c], own_all.at[x, h, c], dev(flip=True), core_o_s, core_o_r)
+    nx_s, nx_r = new_send(norm_all.at[0:3, 0]), new_recv()
+    for k in RING:
+        cols = pl.ds(pl.multiple_of(((x + k) % 4 * 4 + h) * 256, 256), 256)
+        push(norm.at[:, cols], norm_all.at[x, c], dev(dx=k), nx_s, nx_r)
+    norm_all[x, c] = norm[:, pl.ds(pl.multiple_of((x * 4 + h) * 256, 256), 256)]
+
     pick_s, pick_r = new_send(hr), new_recv()
     for k in range(4):
         part = dot(picks, heads[x, k], ((1,), (0,)))
@@ -233,7 +288,8 @@
 
     others_n = others.T.astype(BF16)
     feat_s, feat_r = new_send(fr), [new_recv() for _ in range(4)]
-    for q in range(4):
+
+    def start_feat(q):
         for k in range(4):
             part = dot(others_n, heads[q, k], ((1,), (0,)))
             for yy in range(4):
@@ -243,47 +299,63 @@
         for i, k in enumerate(RING):
             push(fs.at[q, (y + k) % 4], fr.at[q, i], dev(dy=k), feat_s, feat_r[q])
 
+    start_feat(0)
+    expoz_s, expoz_r = new_send(expo_all.at[0, 0:3]), [new_recv() for _ in Z_CLASS]
+    expox_s, expox_r = new_send(expo_all.at[0:3]), [new_recv() for _ in range(4)]
+
+    def spread_expo(j):
+        block = expo_all.at[x, order[j]]
+        if j:
+            wait(expoz_r[j % 3], block)
+        for k in RING:
+            push(block, block, dev(dx=k), expox_s, expox_r[j])
+
+    wait(core_e_r, expo_all.at[0, 0, 0])
+
+    def push_expo(i):
+        push(expo_all.at[x, h], expo_all.at[x, h], dev(dz=Z_CLASS[i]), expoz_s, expoz_r[i])
+
+    push_expo(1)
+    push_expo(2)
+    spread_expo(0)
+    wait(core_o_r, own_all.at[0, 0, 0])
+    ownz_s, ownz_r = new_send(own_all.at[0, 0:3]), new_recv()
+    for k in Z_CLASS:
+        push(own_all.at[x, h], own_all.at[x, h], dev(dz=k), ownz_s, ownz_r)
+    start_feat(1)
     summed_stats = combine(stats_1, stats_r, 15)
     stats_r = send_stats(stats_2, summed_stats, [dev(dz=k) for k in Z_CLASS])
+    push_expo(0)
+    start_feat(2)
+    start_feat(3)
     wait(pick_r, hr)
     hx[x] = (hs[y].astype(F32) + hr[0].astype(F32) + hr[1].astype(F32) + hr[2].astype(F32)).astype(BF16)
     pickx_s, pickx_r = new_send(hx.at[0:3]), new_recv()
     for k in RING:
         push(hx.at[x], hx.at[x], dev(dx=k), pickx_s, pickx_r)
+    wait(nx_r, norm_all.at[0:3, 0])
+    nc_s, nc_r = new_send(norm_all.at[:, 0]), new_recv()
+    push(norm_all.at[:, c], norm_all.at[:, c], dev(flip=True), nc_s, nc_r)
+    wait(ownz_r, own_all.at[0, 0:3])
+    ownx_s, ownx_r = new_send(own_all.at[0:3]), new_recv()
+    for k in RING:
+        push(own_all.at[x], own_all.at[x], dev(dx=k), ownx_s, ownx_r)
+    spread_expo(1)
+    spread_expo(2)
     summed_stats = combine(stats_2, stats_r, 3)
+    plane_all[x, c] = summed_stats
+    core_p_s, core_p_r = new_send(plane_all.at[0, 0]), new_recv()
+    push(plane_all.at[x, c], plane_all.at[x, c], dev(flip=True), core_p_s, core_p_r)
     peak = summed_stats[0:1]
     total = summed_stats[1:2] + summed_stats[2:3]
     scale = weight / total
 
-    dlog = expo * (scale * jnp.exp(first_peak - peak)) - jnp.where(at_target, weight, 0.0)
-    dlog_t[...] = dlog.astype(BF16)
-    dlog_s, dlog_r = new_send(dlog_2.at[0]), new_recv()
-    push(dlog_t.at[other], dlog_2.at[c], dev(flip=True), dlog_s, dlog_r)
-    dlog_2[c] = dlog_t[mine, :]
-    coef[...] = jnp.concatenate(
-        [scale * jnp.exp(stats_1[i][0:1] - peak) for i in (12, 13, 14, 15)]
-        + [scale * summed_stats[1:2], jnp.zeros((123, 128), F32)],
-        axis=0,
-    ).T
-    factors = coef[pl.ds(pl.multiple_of(32 * y, 32), 32), :]
-
-    wait(dlog_r, dlog_2.at[0])
-    wait(norm_r, norm.at[other])
-    dlog_all = jnp.concatenate([dlog_2[0], dlog_2[1]], axis=1)
-    grad_order = [(h + k // 4) % 4 for k in Z_CLASS] + [h]
-    grad_s, grad_r = new_send(gr), [new_recv() for _ in range(4)]
-
-    def start_grad(j):
-        for k in range(4):
-            cols = pl.ds(pl.multiple_of((k * 4 + grad_order[j]) * 256, 256), 256)
-            part = dot(dlog_all, norm[:, cols], ((1,), (0,)))
-            grad[j, k] = part
-            gs[j, k] = part.astype(BF16)
-        for i, k in enumerate(RING):
-            push(gs.at[j, (x + k) % 4], gr.at[j, i], dev(dx=k), grad_s, grad_r[j])
+    wait(core_p_r, plane_all.at[0, 0])
+    px_s, px_r = new_send(plane_all.at[0:3]), new_recv()
+    for k in RING:
+        push(plane_all.at[x], plane_all.at[x], dev(dx=k), px_s, px_r)
 
     swin_s, swin_r = new_send(wr), new_recv()
-    gradz_s, gradz_r = new_send(gs_z), new_recv()
 
     def finish_feat(q):
         wait(feat_r[q], fr.at[q])
@@ -299,34 +371,44 @@
         for i, k in enumerate((1, 15, 2 if q < 2 else 14)):
             push(ws.at[q, (l + k) % 4], wr.at[q, i], dev(dz=k), swin_s, swin_r)
 
-    def finish_grad(j):
-        wait(grad_r[j], gr.at[j])
-        whole = grad[j, x] + gr[j, 0].astype(F32) + gr[j, 1].astype(F32) + gr[j, 2].astype(F32)
-        if j == 3:
-            gq[h] = whole.astype(BF16)
-        else:
-            gs_z[j] = whole.astype(BF16)
-            push(gs_z.at[j], gq.at[h], dev(dz=Z_CLASS[j]), gradz_s, gradz_r)
-
-    start_grad(0)
+    coef[...] = jnp.concatenate(
+        [scale * jnp.exp(stats_1[i][0:1] - peak) for i in (12, 13, 14, 15)]
+        + [scale * summed_stats[1:2], jnp.zeros((123, 128), F32)],
+        axis=0,
+    ).T
+    factors = coef[pl.ds(pl.multiple_of(32 * y, 32), 32), :]
     wait(pickx_r, hx.at[0:3])
     finish_feat(0)
     finish_feat(1)
-    start_grad(1)
     finish_feat(2)
     finish_feat(3)
-    start_grad(2)
-    start_grad(3)
-    for j in range(4):
-        finish_grad(j)
+
+    def grad_block(j):
+        hh = order[j]
+        wait(expox_r[j], expo_all.at[0:3, hh])
+        ids = 512 * dp + 128 * hh + lax.broadcasted_iota(jnp.int32, (128, 256), 0)
+        at_targets = ids == both_targets
+        whole = jnp.zeros((128, 256), F32)
+        for xx in range(4):
+            scales, minus = [], []
+            for core in range(2):
+                plane = plane_all[xx, core]
+                per = lane_weights(xx) / (plane[1:2] + plane[2:3])
+                scales.append(per * jnp.exp(own_all[xx, hh, core, 0:1] - plane[0:1]))
+                minus.append(per * plane[1:2])
+            part = jnp.concatenate([expo_all[xx, hh, core].astype(F32) for core in range(2)], axis=1)
+            part = part * jnp.concatenate(scales, axis=1)
+            part = part - jnp.where(at_targets, jnp.concatenate(minus, axis=1), 0.0)
+            rows = jnp.concatenate([norm_all[xx, core] for core in range(2)], axis=0)
+            whole += dot(part.astype(BF16), rows, ((1,), (0,)))
+        ghead_ref[pl.ds(pl.multiple_of(hh * 128, 128), 128), :] = whole.astype(BF16)
 
     wait(swin_r, wr)
     got = jnp.concatenate(
         [wo[q, l] + wr[q, 0].astype(F32) + wr[q, 1].astype(F32) + wr[q, 2].astype(F32) for q in range(4)],
         axis=1,
     )
-    rows8 = hid8[...]
-    inverse = inv8[:, 0:1]
+    rows8, inverse = rows_of(y, l)
     row_dots = jnp.mean(got * gain * rows8, axis=-1, keepdims=True)
     exits = inverse * (gain * got - rows8 * (inverse * inverse * row_dots))
     later = [None] * 4
@@ -337,6 +419,9 @@
     plane_s, plane_r = new_send(tr), new_recv()
     for i, k in enumerate(RING):
         push(ts, tr.at[i], dev(dx=k), plane_s, plane_r)
+    wait(nc_r, norm_all.at[:, 0])
+    wait(ownx_r, own_all.at[0:3])
+    wait(px_r, plane_all.at[0:3])
     wait(plane_r, tr)
     above = jnp.zeros((2, D), F32)
     for i, k in enumerate(RING):
@@ -348,14 +433,14 @@
     class_s, class_r = new_send(cr), new_recv()
     for i, k in enumerate(Z_CLASS):
         push(cs.at[(h + k // 4) % 4], cr.at[i], dev(dz=k), class_s, class_r)
+    spread_expo(3)
+    for j in range(4):
+        grad_block(j)
     wait(class_r, cr)
     result = sf[h] + top_v[...].astype(F32)
     for i in range(3):
         result += cr[i].astype(F32)
     ghid_ref[0] = result.astype(BF16)
-    wait(gradz_r, gq.at[0:3])
-    for k in range(4):
-        ghead_ref[k * 128 : k * 128 + 128, :] = gq[k]
     assert counts == {"send": SENDS, "recv": RECVS}
     for sem, ref in sent:
         wait(sem, ref)
@@ -373,19 +458,19 @@
         in_specs=[where_it_is] * 6,
         out_specs=(vmem, vmem),
         scratch_shapes=[
-            pltpu.VMEM((4, 2, D), BF16),
+            pltpu.VMEM((4, 4, 4, 2, D), BF16),
             pltpu.VMEM((1, D), F32),
             pltpu.VMEM((2, D), BF16),
-            pltpu.VMEM((8, D), F32),
-            pltpu.VMEM((8, 128), F32),
-            pltpu.VMEM((4, 4, 8, D), BF16),
-            pltpu.VMEM((256, D), BF16),
+            pltpu.VMEM((128, D), BF16),
             pltpu.VMEM((4, 4, 256, 256), BF16),
             pltpu.VMEM((256, 128), F32),
             pltpu.VMEM((16, 8, 128), F32),
             pltpu.VMEM((4, 8, 128), F32),
             pltpu.VMEM((256, 128), BF16),
-            pltpu.VMEM((2, 128, 128), BF16),
+            pltpu.VMEM((4, 4, 2, 128, 128), BF16),
+            pltpu.VMEM((4, 4, 2, 8, 128), F32),
+            pltpu.VMEM((4, 2, 8, 128), F32),
+            pltpu.VMEM((4, 2, 128, 256), BF16),
             pltpu.VMEM((128, 128), F32),
             pltpu.VMEM((4, 8, 1024), BF16),
             pltpu.VMEM((3, 8, 1024), BF16),
@@ -401,11 +486,6 @@
             pltpu.VMEM((4, 2, D), F32),
             pltpu.VMEM((4, 2, D), BF16),
             pltpu.VMEM((3, 2, D), BF16),
-            pltpu.VMEM((4, 4, 128, 256), F32),
-            pltpu.VMEM((4, 4, 128, 256), BF16),
-            pltpu.VMEM((4, 3, 128, 256), BF16),
-            pltpu.VMEM((3, 128, 256), BF16),
-            pltpu.VMEM((4, 128, 256), BF16),
             pltpu.SMEM((64,), jnp.int32),
             pltpu.SMEM((16,), jnp.int32),
             pltpu.SemaphoreType.DMA((SENDS,)),

time: 90.4 us -> 84.4 us (0.934); the launches traced: 90.2 us -> 83.2 us
  Pallas kernels: 87.3 us -> 80.3 us
    pallas_call x1, Pallas kernels: 87.3 us -> 80.3 us  [body(): pl.pallas_call(kernel, out_shape=(jax.ShapeDtypeStruct(exit_head.shape, B...]
where the time goes in v3:
time: 84.4 us; the launch traced here: 83.2 us
  Pallas kernels  80.3 us (95%)
  local copies, waits for them, and re-layouts  2.28 us (3%)
    pallas_call x1, Pallas kernels, body(): pl.pallas_call(kernel, out_shape=(jax.ShapeDtypeStruct(exit_head.shape, B...  80.3 us
    unnamed x4, local copies, waits for them, and re-layouts  2.28 us

profile of v3, /device:TPU:6, one launch (start us, length us, event | category | flops | bytes accessed | tf_op | source)
XLA Modules:
  0.0 83.2 jit_solution(13707536557255529467)
XLA Ops:
  0.6 80.3 %exit_head_backward.1 = (bf16[512,256]{1,0:T(8,128)(2,1)}, bf16[1,2,4096]{2,1,0:T(2,128)(2,1)}) custom-call(bf16[1,2,4096]{2,1,0:T(2,128)(2,1)} %hidden_ref.1, f32[1,4096]{1,0:T(1,128)} %bitcast.1, bf16[512,256]{1,0:T(8,128)(2,1)} %head_ref.1, s32[64]{0:T(128)} %targets_ref.1, s32[16]{0:T(128)} %nums_ref.1, bf16[2,4096]{1,0:T(2,128)(2,1)} %top_ref.1), custom_call_target="tpu_custom_call" | custom-call | tf_op jit(solution)/shard_map/exit_head_backward/pallas_call | solution.py:452
  80.9 0.0 copy-start
  80.9 1.7 %copy.10 = bf16[512,256]{1,0:T(8,128)(2,1)} copy(bf16[512,256]{1,0:T(8,128)(2,1)} %get-tuple-element.4) | data formatting | bytes 524288
  82.6 0.0 copy-done
  82.6 0.6 copy.11
Async XLA Ops:
  80.9 1.7 %copy-start = (bf16[1,2,4096]{2,1,0:T(2,128)(2,1)S(1)}, bf16[1,2,4096]{2,1,0:T(2,128)(2,1)}, u32[]{:S(2)}) copy-start(bf16[1,2,4096]{2,1,0:T(2,128)(2,1)} %get-tuple-element.5) | copy-start | bytes 49156

commit v4 on v3

--- a/solution.py
+++ b/solution.py
@@ -13,8 +13,8 @@
 F32 = jnp.float32
 BF16 = jnp.bfloat16
 D = 4096
-SENDS = 24
-RECVS = 55
+SENDS = 26
+RECVS = 60
 LOCALS = 6
 Z_WINDOW = (1, 15, 2)
 Z_CLASS = (8, 4, 12)
@@ -29,7 +29,7 @@
     hidden_ref, gain_ref, head_ref, targets_ref, nums_ref, top_ref,
     ghead_ref, ghid_ref,
     raw, gain_v, top_v, norm, heads, logits, stats_1, stats_2, expo_t, expo_all, own_all, plane_all, norm_all,
-    coef, hs, hr, hx, feat, fs, fr, wo, ws, wr, ts, tr, sf, cs, cr,
+    coef, hs, hr, hx, hw, hwr, far_top, feat, fs, fr, wo, ws, wr, ts, tr, sf, cs, cr,
     targets_s, nums_s, send_sem, recv_sem, local_sem,
 ):
     sec, dp = lax.axis_index("section"), lax.axis_index("dp")
@@ -66,6 +66,8 @@
 
     mine = pl.ds(pl.multiple_of(c * 128, 128), 128)
     other = pl.ds(pl.multiple_of((1 - c) * 128, 128), 128)
+
+    halves = [pl.ds(pl.multiple_of(c * 128 + 64 * k, 64), 64) for k in range(2)]
 
     def quarter(hh):
         return head_ref.at[pl.ds(pl.multiple_of(hh * 128, 128), 128)]
@@ -113,12 +115,15 @@
 
     to_window(mine_now, raw.at[y, l, h], window_pieces[0])
     to_ring(mine_now, raw.at[y, l, h])
-    headz_s, headz_r = new_send(heads.at[0, 0:3, 0:128]), [new_recv() for _ in Z_CLASS]
+    headz_s, headz_r = new_send(heads.at[0, 0:3, 0:128]), [new_recv() for _ in range(6)]
 
     def transpose(which):
         for i in which:
             k = Z_CLASS[i]
-            push(quarter((h + k // 4) % 4), heads.at[x, h, mine], dev(dz=k), headz_s, headz_r[i])
+            part = (h + k // 4) % 4 * 128
+            for half in range(2):
+                rows = pl.ds(pl.multiple_of(part + 64 * half, 64), 64)
+                push(head_ref.at[rows], heads.at[x, h, halves[half]], dev(dz=k), headz_s, headz_r[2 * i + half])
 
     transpose((1, 2))
     headx_s, headx_r = new_send(heads.at[0:3, :, 0:128]), [new_recv() for _ in range(4)]
@@ -181,15 +186,18 @@
     order = [h] + [(h - k // 4) % 4 for k in Z_CLASS[1:] + Z_CLASS[:1]]
 
     def from_head(j):
-        wait(headz_r[j % 3], heads.at[x, order[j], mine])
-        spread(order[j], headx_r[j])
+        for half in range(2):
+            block = heads.at[x, order[j], halves[half]]
+            wait(headz_r[2 * (j % 3) + half], block)
+            for k in RING:
+                push(block, block, dev(dx=k), headx_s, headx_r[j])
 
     from_window(0, 0)
     from_far(0, 0)
     from_class(1, 1)
     from_class(2, 3)
+    from_class(0, 2)
     transpose((0,))
-    from_class(0, 2)
     from_head(1)
     from_head(2)
     from_window(2, 1)
@@ -237,6 +245,36 @@
     first_peak = jnp.max(values, axis=0, keepdims=True)
     expo = jnp.exp(values - first_peak)
     others = jnp.where(at_target, 0.0, expo)
+    others_n = others.T.astype(BF16)
+    feat_s, feat_r = new_send(fr), [new_recv() for _ in range(4)]
+
+    def start_feat(q):
+        for k in range(4):
+            part = dot(others_n, heads[q, k], ((1,), (0,)))
+            for yy in range(4):
+                rows = part[32 * yy : 32 * yy + 32]
+                feat[q, yy, :, 256 * k : 256 * k + 256] = rows
+                fs[q, yy, :, 256 * k : 256 * k + 256] = rows.astype(BF16)
+        for i, k in enumerate(RING):
+            push(fs.at[q, (y + k) % 4], fr.at[q, i], dev(dy=k), feat_s, feat_r[q])
+
+    start_feat(0)
+
+    expo_t[...] = others.astype(BF16)
+    core_e_s, core_e_r = new_send(expo_all.at[0, 0, 0]), new_recv()
+    push(expo_t.at[other], expo_all.at[x, h, c], dev(flip=True), core_e_s, core_e_r)
+    expo_all[x, h, c] = expo_t[mine, :]
+    expoz_s, expoz_r = new_send(expo_all.at[0, 0:3]), [new_recv() for _ in Z_CLASS]
+    expox_s, expox_r = new_send(expo_all.at[0:3]), [new_recv() for _ in range(4)]
+
+    def spread_expo(j):
+        block = expo_all.at[x, order[j]]
+        if j:
+            wait(expoz_r[j % 3], block)
+        for k in RING:
+            push(block, block, dev(dx=k), expox_s, expox_r[j])
+
+
     own_stats = jnp.concatenate(
         [
             first_peak,
@@ -264,20 +302,14 @@
 
     peers = [dev(dy=i, dz=k) for k in Z_WINDOW + (0,) for i in RING + (0,)][:-1]
     stats_r = send_stats(stats_1, own_stats, peers)
-
-    expo_t[...] = others.astype(BF16)
-    core_e_s, core_e_r = new_send(expo_all.at[0, 0, 0]), new_recv()
-    push(expo_t.at[other], expo_all.at[x, h, c], dev(flip=True), core_e_s, core_e_r)
-    expo_all[x, h, c] = expo_t[mine, :]
-    core_o_s, core_o_r = new_send(own_all.at[0, 0, 0]), new_recv()
-    own_all[x, h, c] = own_stats
-    push(own_all.at[x, h, c], own_all.at[x, h, c], dev(flip=True), core_o_s, core_o_r)
-    nx_s, nx_r = new_send(norm_all.at[0:3, 0]), new_recv()
-    for k in RING:
-        cols = pl.ds(pl.multiple_of(((x + k) % 4 * 4 + h) * 256, 256), 256)
-        push(norm.at[:, cols], norm_all.at[x, c], dev(dx=k), nx_s, nx_r)
-    norm_all[x, c] = norm[:, pl.ds(pl.multiple_of((x * 4 + h) * 256, 256), 256)]
-
+    wait(core_e_r, expo_all.at[0, 0, 0])
+
+    def push_expo(i):
+        push(expo_all.at[x, h], expo_all.at[x, h], dev(dz=Z_CLASS[i]), expoz_s, expoz_r[i])
+
+    push_expo(1)
+    push_expo(2)
+    start_feat(1)
     pick_s, pick_r = new_send(hr), new_recv()
     for k in range(4):
         part = dot(picks, heads[x, k], ((1,), (0,)))
@@ -285,49 +317,25 @@
             hs[yy, :, 256 * k : 256 * k + 256] = part[8 * yy : 8 * yy + 8].astype(BF16)
     for i, k in enumerate(RING):
         push(hs.at[(y + k) % 4], hr.at[i], dev(dy=k), pick_s, pick_r)
-
-    others_n = others.T.astype(BF16)
-    feat_s, feat_r = new_send(fr), [new_recv() for _ in range(4)]
-
-    def start_feat(q):
-        for k in range(4):
-            part = dot(others_n, heads[q, k], ((1,), (0,)))
-            for yy in range(4):
-                rows = part[32 * yy : 32 * yy + 32]
-                feat[q, yy, :, 256 * k : 256 * k + 256] = rows
-                fs[q, yy, :, 256 * k : 256 * k + 256] = rows.astype(BF16)
-        for i, k in enumerate(RING):
-            push(fs.at[q, (y + k) % 4], fr.at[q, i], dev(dy=k), feat_s, feat_r[q])
-
-    start_feat(0)
-    expoz_s, expoz_r = new_send(expo_all.at[0, 0:3]), [new_recv() for _ in Z_CLASS]
-    expox_s, expox_r = new_send(expo_all.at[0:3]), [new_recv() for _ in range(4)]
-
-    def spread_expo(j):
-        block = expo_all.at[x, order[j]]
-        if j:
-            wait(expoz_r[j % 3], block)
-        for k in RING:
-            push(block, block, dev(dx=k), expox_s, expox_r[j])
-
-    wait(core_e_r, expo_all.at[0, 0, 0])
-
-    def push_expo(i):
-        push(expo_all.at[x, h], expo_all.at[x, h], dev(dz=Z_CLASS[i]), expoz_s, expoz_r[i])
-
-    push_expo(1)
-    push_expo(2)
     spread_expo(0)
+    start_feat(2)
+
+    core_o_s, core_o_r = new_send(own_all.at[0, 0, 0]), new_recv()
+    own_all[x, h, c] = own_stats
+    push(own_all.at[x, h, c], own_all.at[x, h, c], dev(flip=True), core_o_s, core_o_r)
+    summed_stats = combine(stats_1, stats_r, 15)
+    stats_r = send_stats(stats_2, summed_stats, [dev(dz=k) for k in Z_CLASS])
+    start_feat(3)
     wait(core_o_r, own_all.at[0, 0, 0])
     ownz_s, ownz_r = new_send(own_all.at[0, 0:3]), new_recv()
     for k in Z_CLASS:
         push(own_all.at[x, h], own_all.at[x, h], dev(dz=k), ownz_s, ownz_r)
-    start_feat(1)
-    summed_stats = combine(stats_1, stats_r, 15)
-    stats_r = send_stats(stats_2, summed_stats, [dev(dz=k) for k in Z_CLASS])
     push_expo(0)
-    start_feat(2)
-    start_feat(3)
+    nx_s, nx_r = new_send(norm_all.at[0:3, 0]), new_recv()
+    for k in RING:
+        cols = pl.ds(pl.multiple_of(((x + k) % 4 * 4 + h) * 256, 256), 256)
+        push(norm.at[:, cols], norm_all.at[x, c], dev(dx=k), nx_s, nx_r)
+    norm_all[x, c] = norm[:, pl.ds(pl.multiple_of((x * 4 + h) * 256, 256), 256)]
     wait(pick_r, hr)
     hx[x] = (hs[y].astype(F32) + hr[0].astype(F32) + hr[1].astype(F32) + hr[2].astype(F32)).astype(BF16)
     pickx_s, pickx_r = new_send(hx.at[0:3]), new_recv()
@@ -336,12 +344,48 @@
     wait(nx_r, norm_all.at[0:3, 0])
     nc_s, nc_r = new_send(norm_all.at[:, 0]), new_recv()
     push(norm_all.at[:, c], norm_all.at[:, c], dev(flip=True), nc_s, nc_r)
-    wait(ownz_r, own_all.at[0, 0:3])
-    ownx_s, ownx_r = new_send(own_all.at[0:3]), new_recv()
-    for k in RING:
-        push(own_all.at[x], own_all.at[x], dev(dx=k), ownx_s, ownx_r)
+    tops = [
+        functools.reduce(jnp.maximum, [stats_1[4 * i + k][0:1] for k in range(4)]) for i in range(4)
+    ]
+
+    far_s, far_r = new_send(far_top.at[0]), new_recv()
+    far_top[0] = jnp.broadcast_to(tops[3], (8, 128))
+    push(far_top.at[0], far_top.at[1], dev(dz=14), far_s, far_r)
+
+    def as_rows(lanes, at, size):
+        blank = jnp.zeros((128 - len(lanes), 128), F32)
+        coef[...] = jnp.concatenate(lanes + [blank], axis=0).T
+        return coef[pl.ds(pl.multiple_of(at, size), size), :]
+
+    shares = as_rows([jnp.exp(stats_1[12 + i][0:1] - tops[3]) for i in range(4)], 32 * y, 32)
+    swin_s, swin_r = new_send(wr), new_recv()
+
+    def finish_feat(q):
+        wait(feat_r[q], fr.at[q])
+        summed = shares[:, 3:4] * feat[q, y]
+        for i in range(3):
+            summed += shares[:, i : i + 1] * fr[q, i].astype(F32)
+        for k in range(4):
+            wo[q, k] = summed[8 * k : 8 * k + 8]
+            ws[q, k] = summed[8 * k : 8 * k + 8].astype(BF16)
+        for i, k in enumerate((1, 15, 2 if q < 2 else 14)):
+            push(ws.at[q, (l + k) % 4], wr.at[q, i], dev(dz=k), swin_s, swin_r)
+
+    wait(pickx_r, hx.at[0:3])
+    picked = jnp.concatenate([hx[q].astype(F32) for q in range(4)], axis=1)
+    for k in range(4):
+        hw[k] = picked[2 * k : 2 * k + 2].astype(BF16)
+    hw_s, hw_r = new_send(hwr), new_recv()
+    for i, k in enumerate((1, 15)):
+        push(hw.at[(l + k) % 4], hwr.at[i], dev(dz=k), hw_s, hw_r)
+    for k, cols in ((2, cols_a), (14, cols_b)):
+        push(hw.at[(l + 2) % 4, :, cols], hwr.at[2, :, cols], dev(dz=k), hw_s, hw_r)
+    finish_feat(0)
     spread_expo(1)
     spread_expo(2)
+    finish_feat(1)
+    finish_feat(2)
+    finish_feat(3)
     summed_stats = combine(stats_2, stats_r, 3)
     plane_all[x, c] = summed_stats
     core_p_s, core_p_r = new_send(plane_all.at[0, 0]), new_recv()
@@ -355,33 +399,9 @@
     for k in RING:
         push(plane_all.at[x], plane_all.at[x], dev(dx=k), px_s, px_r)
 
-    swin_s, swin_r = new_send(wr), new_recv()
-
-    def finish_feat(q):
-        wait(feat_r[q], fr.at[q])
-        summed = factors[:, 3:4] * feat[q, y]
-        for i in range(3):
-            summed += factors[:, i : i + 1] * fr[q, i].astype(F32)
-        rows = hx[q].astype(F32)
-        rows = jnp.concatenate([rows[2 * (k // 4) : 2 * (k // 4) + 2] for k in range(16)], axis=0)
-        summed -= factors[:, 4:5] * rows
-        for k in range(4):
-            wo[q, k] = summed[8 * k : 8 * k + 8]
-            ws[q, k] = summed[8 * k : 8 * k + 8].astype(BF16)
-        for i, k in enumerate((1, 15, 2 if q < 2 else 14)):
-            push(ws.at[q, (l + k) % 4], wr.at[q, i], dev(dz=k), swin_s, swin_r)
-
-    coef[...] = jnp.concatenate(
-        [scale * jnp.exp(stats_1[i][0:1] - peak) for i in (12, 13, 14, 15)]
-        + [scale * summed_stats[1:2], jnp.zeros((123, 128), F32)],
-        axis=0,
-    ).T
-    factors = coef[pl.ds(pl.multiple_of(32 * y, 32), 32), :]
-    wait(pickx_r, hx.at[0:3])
-    finish_feat(0)
-    finish_feat(1)
-    finish_feat(2)
-    finish_feat(3)
+    wait(far_r, far_top.at[1])
+    spreads = [scale * jnp.exp(top - peak) for top in tops + [far_top[1, 0:1]]]
+    factors = as_rows(spreads + [scale * summed_stats[1:2]], 32 * y + 8 * l, 8)
 
     def grad_block(j):
         hh = order[j]
@@ -404,10 +424,16 @@
         ghead_ref[pl.ds(pl.multiple_of(hh * 128, 128), 128), :] = whole.astype(BF16)
 
     wait(swin_r, wr)
-    got = jnp.concatenate(
-        [wo[q, l] + wr[q, 0].astype(F32) + wr[q, 1].astype(F32) + wr[q, 2].astype(F32) for q in range(4)],
-        axis=1,
-    )
+    wait(hw_r, hwr)
+    got = factors[:, 3:4] * jnp.concatenate([wo[q, l] for q in range(4)], axis=1)
+    for i in range(3):
+        halves_in = [jnp.concatenate([wr[q, i], wr[q + 1, i]], axis=1).astype(F32) for q in (0, 2)]
+        later_one = 4 if i == 2 else i
+        got += jnp.concatenate(
+            [factors[:, i : i + 1] * halves_in[0], factors[:, later_one : later_one + 1] * halves_in[1]], axis=1
+        )
+    rows2 = hw[l].astype(F32) + hwr[0].astype(F32) + hwr[1].astype(F32) + hwr[2].astype(F32)
+    got -= factors[:, 5:6] * jnp.concatenate([rows2] * 4, axis=0)
     rows8, inverse = rows_of(y, l)
     row_dots = jnp.mean(got * gain * rows8, axis=-1, keepdims=True)
     exits = inverse * (gain * got - rows8 * (inverse * inverse * row_dots))
@@ -419,9 +445,6 @@
     plane_s, plane_r = new_send(tr), new_recv()
     for i, k in enumerate(RING):
         push(ts, tr.at[i], dev(dx=k), plane_s, plane_r)
-    wait(nc_r, norm_all.at[:, 0])
-    wait(ownx_r, own_all.at[0:3])
-    wait(px_r, plane_all.at[0:3])
     wait(plane_r, tr)
     above = jnp.zeros((2, D), F32)
     for i, k in enumerate(RING):
@@ -433,7 +456,14 @@
     class_s, class_r = new_send(cr), new_recv()
     for i, k in enumerate(Z_CLASS):
         push(cs.at[(h + k // 4) % 4], cr.at[i], dev(dz=k), class_s, class_r)
+    wait(ownz_r, own_all.at[0, 0:3])
+    ownx_s, ownx_r = new_send(own_all.at[0:3]), new_recv()
+    for k in RING:
+        push(own_all.at[x], own_all.at[x], dev(dx=k), ownx_s, ownx_r)
     spread_expo(3)
+    wait(nc_r, norm_all.at[:, 0])
+    wait(ownx_r, own_all.at[0:3])
+    wait(px_r, plane_all.at[0:3])
     for j in range(4):
         grad_block(j)
     wait(class_r, cr)
@@ -475,6 +505,9 @@
             pltpu.VMEM((4, 8, 1024), BF16),
             pltpu.VMEM((3, 8, 1024), BF16),
             pltpu.VMEM((4, 8, 1024), BF16),
+            pltpu.VMEM((4, 2, D), BF16),
+            pltpu.VMEM((3, 2, D), BF16),
+            pltpu.VMEM((2, 8, 128), F32),
             pltpu.VMEM((4, 4, 32, 1024), F32),
             pltpu.VMEM((4, 4, 32, 1024), BF16),
             pltpu.VMEM((4, 3, 32, 1024), BF16),

time: 84.4 us -> 81.9 us (0.970)
  Pallas kernels: 80.3 us -> 78.3 us
    pallas_call x1, Pallas kernels: 80.3 us -> 78.3 us  [body(): pl.pallas_call(kernel, out_shape=(jax.ShapeDtypeStruct(exit_head.shape, B...]
where the time goes in v4:
time: 81.9 us; the launch traced here: 81.2 us
  Pallas kernels  78.3 us (96%)
  local copies, waits for them, and re-layouts  2.28 us (3%)
    pallas_call x1, Pallas kernels, body(): pl.pallas_call(kernel, out_shape=(jax.ShapeDtypeStruct(exit_head.shape, B...  78.3 us
    unnamed x4, local copies, waits for them, and re-layouts  2.28 us

profile of v4, /device:TPU:6, one launch (start us, length us, event | category | flops | bytes accessed | tf_op | source)
XLA Modules:
  0.0 81.2 jit_solution(17523590419621663124)
XLA Ops:
  0.6 78.3 %exit_head_backward.1 = (bf16[512,256]{1,0:T(8,128)(2,1)}, bf16[1,2,4096]{2,1,0:T(2,128)(2,1)}) custom-call(bf16[1,2,4096]{2,1,0:T(2,128)(2,1)} %hidden_ref.1, f32[1,4096]{1,0:T(1,128)} %bitcast.1, bf16[512,256]{1,0:T(8,128)(2,1)} %head_ref.1, s32[64]{0:T(128)} %targets_ref.1, s32[16]{0:T(128)} %nums_ref.1, bf16[2,4096]{1,0:T(2,128)(2,1)} %top_ref.1), custom_call_target="tpu_custom_call" | custom-call | tf_op jit(solution)/shard_map/exit_head_backward/pallas_call | solution.py:482
  78.9 0.0 copy-start
  78.9 1.7 %copy.10 = bf16[512,256]{1,0:T(8,128)(2,1)} copy(bf16[512,256]{1,0:T(8,128)(2,1)} %get-tuple-element.4) | data formatting | bytes 524288
  80.6 0.0 copy-done
  80.6 0.6 copy.11
Async XLA Ops:
  78.9 1.7 %copy-start = (bf16[1,2,4096]{2,1,0:T(2,128)(2,1)S(1)}, bf16[1,2,4096]{2,1,0:T(2,128)(2,1)}, u32[]{:S(2)}) copy-start(bf16[1,2,4096]{2,1,0:T(2,128)(2,1)} %get-tuple-element.5) | copy-start | bytes 49156

commit v5 on v4

--- a/solution.py
+++ b/solution.py
@@ -125,7 +125,6 @@
                 rows = pl.ds(pl.multiple_of(part + 64 * half, 64), 64)
                 push(head_ref.at[rows], heads.at[x, h, halves[half]], dev(dz=k), headz_s, headz_r[2 * i + half])
 
-    transpose((1, 2))
     headx_s, headx_r = new_send(heads.at[0:3, :, 0:128]), [new_recv() for _ in range(4)]
 
     def spread(hh, sem):
@@ -192,6 +191,7 @@
             for k in RING:
                 push(block, block, dev(dx=k), headx_s, headx_r[j])
 
+    transpose((1, 2))
     from_window(0, 0)
     from_far(0, 0)
     from_class(1, 1)

time: 81.9 us -> 81.9 us (level)
  no operation moved by 1% of the time
where the time goes in v5:
time: 81.9 us; the launch traced here: 81.2 us
  Pallas kernels  78.3 us (96%)
  local copies, waits for them, and re-layouts  2.28 us (3%)
    pallas_call x1, Pallas kernels, body(): pl.pallas_call(kernel, out_shape=(jax.ShapeDtypeStruct(exit_head.shape, B...  78.3 us
    unnamed x4, local copies, waits for them, and re-layouts  2.28 us

profile of v5, /device:TPU:6, one launch (start us, length us, event | category | flops | bytes accessed | tf_op | source)
XLA Modules:
  0.0 81.2 jit_solution(8770340042118824784)
XLA Ops:
  0.6 78.3 %exit_head_backward.1 = (bf16[512,256]{1,0:T(8,128)(2,1)}, bf16[1,2,4096]{2,1,0:T(2,128)(2,1)}) custom-call(bf16[1,2,4096]{2,1,0:T(2,128)(2,1)} %hidden_ref.1, f32[1,4096]{1,0:T(1,128)} %bitcast.1, bf16[512,256]{1,0:T(8,128)(2,1)} %head_ref.1, s32[64]{0:T(128)} %targets_ref.1, s32[16]{0:T(128)} %nums_ref.1, bf16[2,4096]{1,0:T(2,128)(2,1)} %top_ref.1), custom_call_target="tpu_custom_call" | custom-call | tf_op jit(solution)/shard_map/exit_head_backward/pallas_call | solution.py:482
  78.9 0.0 copy-start
  78.9 1.7 %copy.10 = bf16[512,256]{1,0:T(8,128)(2,1)} copy(bf16[512,256]{1,0:T(8,128)(2,1)} %get-tuple-element.4) | data formatting | bytes 524288
  80.6 0.0 copy-done
  80.6 0.6 copy.11
Async XLA Ops:
  78.9 1.7 %copy-start = (bf16[1,2,4096]{2,1,0:T(2,128)(2,1)S(1)}, bf16[1,2,4096]{2,1,0:T(2,128)(2,1)}, u32[]{:S(2)}) copy-start(bf16[1,2,4096]{2,1,0:T(2,128)(2,1)} %get-tuple-element.5) | copy-start | bytes 49156
